TPU v7x, 128 devices: a whole 4x4x4 slice. The times are simulated.
128 devices in a mesh: tm: 16 (over y, z), rows: 8 (over x, core).
Axes of the slice: x: 4, y: 4, z: 4, core: 2. Of those that a mesh axis runs over, the one named last changes fastest.
Arguments:
- video: bfloat16 [128, 64, 128, 128], P('tm', 'rows'), may hold values from -6 to 6
- w_space: bfloat16 [3, 3, 128, 128], replicated, may hold values from -0.1875 to 0.1875
- w_time: bfloat16 [3, 128, 128], replicated, may hold values from -0.3125 to 0.3125
- w_pixel: bfloat16 [3, 128], replicated, may hold values from -0.5 to 0.5
- w_patch: bfloat16 [192, 256], replicated, may hold values from -0.4375 to 0.4375
- w_logit: bfloat16 [256], replicated, may hold values from -0.375 to 0.375
- grad_out: bfloat16 [128, 64, 128, 128], P('tm', 'rows'), may hold values from -6 to 6
Outputs:
- input_grad: bfloat16 [128, 64, 128, 128], P('tm', 'rows')
- space_grad: float32 [3, 3, 128, 128], replicated
- time_grad: float32 [3, 128, 128], replicated
- logits: float32 [128, 8, 16], P(('tm', 'rows'))
All inputs are finite; a program needn't handle non-finite values.
Results may differ from a plain program's by a relative error of at most 0.008.
Values may be sent and summed in bfloat16 or wider, within the bound.
A program may use at most 128 MiB of HBM per device.

v0:
```python
import math

import jax
import jax.numpy as jnp
from jax import lax
from jax.sharding import PartitionSpec as P

PATCH = 8


def extended(cells, sides, width):
    for axis, dim in sides:
        count = lax.axis_size(axis)
        ends = count - 1
        head = lax.slice_in_dim(cells, 0, width, axis=dim)
        tail = lax.slice_in_dim(cells, cells.shape[dim] - width, cells.shape[dim], axis=dim)
        cells = jnp.concatenate(
            [
                lax.ppermute(tail, axis, [(i, (i + 1) % count) for i in range(ends)]),
                cells,
                lax.ppermute(head, axis, [((i + 1) % count, i) for i in range(ends)]),
            ],
            axis=dim,
        )
    return cells


def passed_along(block, axis, distance):
    devices = range(lax.axis_size(axis))
    route = [(i - distance, i) for i in devices if i - distance in devices]
    return lax.ppermute(block, axis, route)


def column_stack(padded, row_start, rows, width):
    parts = [padded[:, row_start : row_start + rows, col : col + width] for col in range(3)]
    joined = jnp.concatenate(parts, axis=-1)
    return joined.reshape(-1, joined.shape[-1])


def judge_scaled(pixels, center, factor, w_patch, w_logit):
    values = pixels.astype(jnp.float32)
    normed = ((values - center) * factor).astype(jnp.bfloat16)
    count, height, colours, width = normed.shape
    tiles = normed.reshape(count, height // PATCH, PATCH, colours, width // PATCH, PATCH)
    tiles = tiles.transpose(0, 1, 4, 2, 3, 5).reshape(-1, colours * PATCH * PATCH)
    inner = jax.nn.leaky_relu(jnp.dot(tiles, w_patch, preferred_element_type=jnp.float32), 0.2)
    return jnp.dot(inner, w_logit.astype(jnp.float32)).reshape(
        count, height // PATCH, width // PATCH
    )


def shards(video, w_space, w_time, w_pixel, w_patch, w_logit, grad_out):
    frames_dev, rows_dev, width, chans = video.shape
    count = frames_dev * rows_dev * width
    groups = lax.axis_size("rows")
    space_w = w_space.reshape(3, 3 * chans, chans)
    row_pad = extended(video, (("rows", 1),), 1)
    padded = jnp.pad(row_pad, ((0, 0), (0, 0), (1, 1), (0, 0)))
    stacks = [column_stack(padded, start, rows_dev, width) for start in range(3)]
    pre_act = jnp.dot(stacks[0], space_w[0], preferred_element_type=jnp.float32)
    pre_act = pre_act + jnp.dot(stacks[1], space_w[1], preferred_element_type=jnp.float32)
    pre_act = pre_act + jnp.dot(stacks[2], space_w[2], preferred_element_type=jnp.float32)
    hidden = jax.nn.silu(pre_act).astype(jnp.bfloat16).reshape(frames_dev, rows_dev, width, chans)
    earlier = passed_along(hidden[frames_dev - 2 :], "tm", 1)
    history = jnp.concatenate([earlier, hidden], axis=0)
    lagged = jnp.concatenate(
        [history[2:], history[1 : frames_dev + 1], history[0:frames_dev]], axis=-1
    ).reshape(count, 3 * chans)
    temporal = jnp.dot(lagged, w_time.reshape(3 * chans, chans), preferred_element_type=jnp.float32)
    block = (video.reshape(count, chans).astype(jnp.float32) + temporal).astype(jnp.bfloat16)
    block = block.reshape(frames_dev, rows_dev, width, chans)
    pixels = jnp.einsum("frwc,kc->frkw", block, w_pixel, preferred_element_type=jnp.float32).astype(
        jnp.bfloat16
    )
    grouped = pixels.reshape(groups, frames_dev // groups, rows_dev, 3, width)
    single = lax.all_to_all(grouped, "rows", split_axis=0, concat_axis=2, tiled=True)[0]
    values = single.astype(jnp.float32)
    center = jnp.mean(values, axis=(1, 2, 3), keepdims=True)
    spread = jnp.mean((values - center) * (values - center), axis=(1, 2, 3), keepdims=True)
    judged = judge_scaled(single, center, lax.rsqrt(spread + 1e-05), w_patch, w_logit)[None]
    logits = judged.reshape(frames_dev // groups, judged.shape[2], judged.shape[3])
    flat_grad = grad_out.reshape(count, chans)
    contract = (((0,), (0,)), ((), ()))
    time_term = lax.dot_general(
        lagged, flat_grad, contract, preferred_element_type=jnp.float32
    ).reshape(3, chans, chans)
    later = passed_along(grad_out[:2], "tm", -1)
    future = jnp.concatenate([grad_out, later], axis=0)
    leading = jnp.concatenate(
        [future[0:frames_dev], future[1 : frames_dev + 1], future[2 : frames_dev + 2]], axis=-1
    ).reshape(count, 3 * chans)
    time_back = jnp.transpose(w_time, (0, 2, 1)).reshape(3 * chans, chans)
    back_hidden = jnp.dot(leading, time_back, preferred_element_type=jnp.float32)
    sigma = jax.nn.sigmoid(pre_act)
    back_pre = (back_hidden * sigma * (1.0 + pre_act * (1.0 - sigma))).astype(jnp.bfloat16)
    space_term = jnp.stack(
        [
            lax.dot_general(stacks[start], back_pre, contract, preferred_element_type=jnp.float32)
            for start in range(3)
        ]
    )
    space_term = space_term.reshape(3, 3, chans, chans)
    back_rows = extended(back_pre.reshape(frames_dev, rows_dev, width, chans), (("rows", 1),), 1)
    back_pad = jnp.pad(back_rows, ((0, 0), (0, 0), (1, 1), (0, 0)))
    total = flat_grad.astype(jnp.float32)
    for row_off in range(3):
        parts = [
            back_pad[:, 2 - row_off : 2 - row_off + rows_dev, 2 - col_off : 2 - col_off + width]
            for col_off in range(3)
        ]
        joined = jnp.concatenate(parts, axis=-1).reshape(count, 3 * chans)
        kernel = jnp.concatenate([w_space[row_off, col_off].T for col_off in range(3)], axis=0)
        total = total + jnp.dot(joined, kernel, preferred_element_type=jnp.float32)
    input_grad = total.astype(jnp.bfloat16).reshape(frames_dev, rows_dev, width, chans)
    time_sum, space_sum = lax.psum((time_term, space_term), ("tm", "rows"))
    factor = 1.0 / math.sqrt(count * lax.axis_size("tm") * groups)
    return (input_grad, space_sum * factor, time_sum * factor, logits)


def solution(mesh):
    in_specs = (P("tm", "rows", None, None), P(), P(), P(), P(), P(), P("tm", "rows", None, None))
    out_specs = (P("tm", "rows", None, None), P(), P(), P(("tm", "rows"), None, None))
    return jax.shard_map(shards, mesh=mesh, in_specs=in_specs, out_specs=out_specs, check_vma=False)
```

profile of v0, /device:TPU:1, one launch (start us, length us, event | category | flops | bytes accessed | tf_op | source)
XLA Modules:
  0.0 301.9 jit_solution(4312095625495849331)
XLA Ops:
  7.2 2.0 fusion.73
  9.3 4.5 %collective-permute-start.1 = (bf16[8,1,128,128]{3,2,1,0:T(8,128)(2,1)}, bf16[8,1,128,128]{3,2,1,0:T(8,128)(2,1)S(1)}, u32[]{:S(2)}, u32[]{:S(2)}) collective-permute-start(bf16[8,1,128,128]{3,2,1,0:T(8,128)(2,1)} %get-tuple-element.30), channel_id=1, source_target_pairs={{0,1},{1,2},{2,3},{3,4},{4,5},{5,6},{6,7},{8,9},{9,10},{10,11},{11... | collective-permute-start | bytes 786440 | tf_op jit(solution)/shard_map/ppermute | solution.py:19
  13.8 1.9 collective-permute-start.2
  15.7 1.9 slice.132
  20.5 3.2 %constant_dynamic-update-slice_fusion.1 = bf16[10,8,128,128]{3,2,1,0:T(8,128)(2,1)} fusion(bf16[8,8,128,128]{3,2,1,0:T(8,128)(2,1)} %param.13), kind=kLoop, calls=%fused_computation.97 | loop fusion | bytes 4194304
  27.3 2.9 fusion.70
  30.2 6.7 %fusion.9 = (bf16[8,8,128,384]{3,2,1,0:T(8,128)(2,1)}, bf16[8,8,128,384]{3,2,1,0:T(8,128)(2,1)}, bf16[8,8,128,384]{3,2,1,0:T(8,128)(2,1)}) fusion(bf16[8,1,128,128]{3,2,1,0:T(8,128)(2,1)S(1)} %collective-permute-done.2, bf16[8,8,128,128]{3,2,1,0:T(8,128)(2,1)S(1)} %copy-done.5, bf16[8,8,128,128]{3,2,1,0:T(8,128)(2,1)S(1)} %get-tuple-element.17, ...), kind=kLoop, calls=%fused_computation.21 | loop fusion | flops 69206016 | bytes 34078720 | tf_op jit(solution)/shard_map/concatenate | solution.py:36
  36.8 8.6 %copy.23 = bf16[8192,384]{0,1:T(8,128)(2,1)} copy(bf16[8192,384]{1,0:T(8,128)(2,1)} %bitcast.136) | data formatting | bytes 12582912 | tf_op jit(solution)/shard_map/reshape | solution.py:37
  45.4 6.5 %fusion.77 = f32[8192,128]{1,0:T(8,128)} fusion(bf16[8192,384]{1,0:T(8,128)(2,1)} %bitcast.137, bf16[384,128]{1,0:T(8,128)(2,1)S(1)} %bitcast.174), kind=kOutput, calls=%fused_computation.112 | convolution fusion | flops 805306368 | bytes 10584064 | tf_op jit(solution)/shard_map/dot_general | solution.py:60
  52.0 8.6 %copy.24 = bf16[8192,384]{0,1:T(8,128)(2,1)} copy(bf16[8192,384]{1,0:T(8,128)(2,1)} %bitcast.134) | data formatting | bytes 12582912 | tf_op jit(solution)/shard_map/reshape | solution.py:37
  60.6 8.7 %copy.25 = bf16[8192,384]{0,1:T(8,128)(2,1)} copy(bf16[8192,384]{1,0:T(8,128)(2,1)} %bitcast.154) | data formatting | bytes 12582912 | tf_op jit(solution)/shard_map/reshape | solution.py:37
  69.3 6.0 %convolution_add_fusion.5 = f32[8192,128]{1,0:T(8,128)S(1)} fusion(f32[8192,128]{1,0:T(8,128)} %fusion.77, bf16[8192,384]{1,0:T(8,128)(2,1)} %bitcast.135, bf16[384,128]{1,0:T(8,128)(2,1)S(1)} %bitcast.173), kind=kOutput, calls=%fused_computation.5 | convolution fusion | flops 806354944 | bytes 14778368 | tf_op jit(solution)/shard_map/dot_general | solution.py:61
  75.3 4.1 %multiply_convert_fusion = (bf16[8192,128]{1,0:T(8,128)(2,1)S(1)}, f32[8192,128]{1,0:T(8,128)}) fusion(f32[8192,128]{1,0:T(8,128)S(1)} %convolution_add_fusion.5, bf16[8192,384]{1,0:T(8,128)(2,1)S(1)} %bitcast.157, bf16[384,128]{1,0:T(8,128)(2,1)S(1)} %bitcast.175), kind=kOutput, calls=%fused_computation.34 | convolution fusion | flops 811597824 | bytes 16875520 | tf_op jit(solution)/shard_map/dot_general | solution.py:62
  80.3 5.0 %collective-permute-start.5 = (bf16[2,8,128,128]{3,2,1,0:T(8,128)(2,1)}, bf16[2,8,128,128]{3,2,1,0:T(8,128)(2,1)}, u32[]{:S(2)}, u32[]{:S(2)}) collective-permute-start(bf16[2,8,128,128]{3,2,1,0:T(8,128)(2,1)} %bitcast.44), channel_id=1, source_target_pairs={{0,8},{8,16},{16,24},{24,32},{32,40},{40,48},{48,56},{56,64},{64,7... | collective-permute-start | bytes 1572872 | tf_op jit(solution)/shard_map/ppermute | solution.py:31
  86.9 4.1 %pad_maximum_fusion.4 = bf16[8,8,128,384]{3,2,1,0:T(8,128)(2,1)} fusion(bf16[8,8,128,128]{3,2,1,0:T(8,128)(2,1)S(1)} %get-tuple-element.21, bf16[8,8,128,128]{3,2,1,0:T(8,128)(2,1)S(1)} %get-tuple-element.20, bf16[8,8,128,128]{3,2,1,0:T(8,128)(2,1)S(1)} %copy-done.1), kind=kLoop, calls=%fused_computation.25 | loop fusion | flops 18874368 | bytes 12582912 | tf_op jit(solution)/shard_map/concatenate | solution.py:89
  91.1 6.5 %fusion.1 = bf16[8192,128]{1,0:T(8,128)(2,1)S(1)} fusion(bf16[8192,384]{1,0:T(8,128)(2,1)} %bitcast.167, bf16[384,128]{1,0:T(8,128)(2,1)S(1)} %bitcast.177, f32[8192,128]{1,0:T(8,128)} %get-tuple-element.44), kind=kOutput, calls=%fused_computation.8 | convolution fusion | flops 814743552 | bytes 12681216 | tf_op jit(solution)/shard_map/dot_general | solution.py:93
  97.6 1.8 fusion.31
  101.3 4.0 %collective-permute-start.3 = (bf16[8,1,128,128]{3,2,1,0:T(8,128)(2,1)S(1)}, bf16[8,1,128,128]{3,2,1,0:T(8,128)(2,1)S(1)}, u32[]{:S(2)}, u32[]{:S(2)}) collective-permute-start(bf16[8,1,128,128]{3,2,1,0:T(8,128)(2,1)S(1)} %get-tuple-element.24), channel_id=1, source_target_pairs={{0,1},{1,2},{2,3},{3,4},{4,5},{5,6},{6,7},{8,9},{9,10},{10,11},{11... | collective-permute-start | bytes 786440 | tf_op jit(solution)/shard_map/ppermute | solution.py:19
  105.3 1.9 collective-permute-start.4
  107.3 1.8 fusion.37
  111.5 3.4 %fusion.23 = bf16[384,8192]{0,1:T(8,128)(2,1)} fusion(bf16[8192,128]{1,0:T(8,128)(2,1)S(1)} %bitcast.165, bf16[8192,128]{1,0:T(8,128)(2,1)S(1)} %bitcast.163, bf16[8192,128]{1,0:T(8,128)(2,1)S(1)} %copy-done.8), kind=kLoop, calls=%fused_computation.45 | loop fusion | flops 18874368 | bytes 12582912 | tf_op jit(solution)/shard_map/dot_general | solution.py:84
  114.9 2.0 fusion.3
  118.2 4.9 %all-to-all-start = ((bf16[8,1,8,3,128]{4,2,3,1,0:T(8,128)(2,1)}), bf16[8,1,8,3,128]{4,2,3,1,0:T(8,128)(2,1)S(1)}, u32[]{:S(2)}, u32[]{:S(2)}) async-start(bf16[8,1,8,3,128]{4,2,3,1,0:T(8,128)(2,1)} %copy.27), calls=%async_computation | async-start | bytes 98304 | tf_op jit(solution)/shard_map/all_to_all | solution.py:76
  123.2 8.6 %copy.26 = bf16[384,8192]{1,0:T(8,128)(2,1)} copy(bf16[384,8192]{0,1:T(8,128)(2,1)} %fusion.23) | data formatting | bytes 12582912 | tf_op jit(solution)/shard_map/dot_general | solution.py:84
  133.0 5.6 %fusion.69 = (bf16[8,8,128,128]{3,2,1,0:T(8,128)(2,1)}, bf16[8,8,128,128]{3,2,1,0:T(8,128)(2,1)}, bf16[8,8,128,128]{3,2,1,0:T(8,128)(2,1)}, bf16[8,8,128,128]{3,...) fusion(bf16[8,10,130,128]{3,2,1,0:T(8,128)(2,1)S(1)} %select_maximum_fusion), kind=kLoop, calls=%fused_computation.105 | loop fusion | bytes 25165824 | tf_op jit(solution)/shard_map/slice | solution.py:108
  138.6 2.5 fusion.78
  141.1 4.8 %fusion.5 = (bf16[8,8,128,384]{3,2,1,0:T(8,128)(2,1)S(1)}, bf16[8,8,128,384]{3,2,1,0:T(8,128)(2,1)S(1)}) fusion(bf16[8,8,128,128]{3,2,1,0:T(8,128)(2,1)S(1)} %bitcast.140, bf16[8,1,128,128]{3,2,1,0:T(8,128)(2,1)S(1)} %collective-permute-done.3, bf16[8,8,128,128]{3,2,1,0:T(8,128)(2,1)} %get-tuple-element.11, bf16[8,8,128,128]{3,2,1,0:T(8,128)(2,1)} %get-tuple-element.6, ...), kind=kLoop, calls=%fused_computation.15 | loop fusion | flops 50331648 | bytes 23592960 | tf_op jit(solution)/shard_map/concatenate | solution.py:111
  146.1 1.9 convolution_add_fusion.3
  148.3 1.9 convolution_add_fusion.2
  150.1 3.2 %fusion.2 = bf16[8192,128]{1,0:T(8,128)(2,1)} fusion(f32[8192,128]{1,0:T(8,128)S(1)} %convolution_add_fusion.2, bf16[8192,384]{1,0:T(8,128)(2,1)S(1)} %bitcast.143, bf16[128,128]{0,1:T(8,128)(2,1)S(1)} %copy-done.15, bf16[128,128]{0,1:T(8,128)(2,1)S(1)} %copy-done.16, bf16[128,128]{0,1:T(8,128)(2,1)S(1)} %copy-done.14), kind=kOutput, calls=%fused_computation.9 | convolution fusion | flops 807698432 | bytes 12681216 | tf_op jit(solution)/shard_map/dot_general | solution.py:113
  158.5 133.0 %all-reduce.5.cloned.1.call-done = (f32[3,3,128,128]{3,2,1,0:T(8,128)}, f32[3,128,128]{2,1,0:T(8,128)}) async-done(((f32[3,3,128,128]{3,2,1,0:T(8,128)}, f32[3,128,128]{2,1,0:T(8,128)}), (f32[3,3,128,128]{3,2,1,0:T(8,128)}, f32[3,128,128]{2,1,0:T(8,128)})) %all-reduce.5.cloned.1.call-update) | async-done | bytes 786448 | tf_op jit(solution)/shard_map/psum | solution.py:115
  291.5 1.9 broadcast_multiply_fusion
  (115 shorter events, 21.5 us)
Async XLA Ops:
  7.2 150.4 %copy-start = (bf16[192,256]{1,0:T(8,128)(2,1)S(1)}, bf16[192,256]{1,0:T(8,128)(2,1)}, u32[]{:S(2)}) copy-start(bf16[192,256]{1,0:T(8,128)(2,1)} %param.11) | copy-start | bytes 294916
  7.2 18.9 %copy-start.5 = (bf16[8,8,128,128]{3,2,1,0:T(8,128)(2,1)S(1)}, bf16[8,8,128,128]{3,2,1,0:T(8,128)(2,1)}, u32[]{:S(2)}) copy-start(bf16[8,8,128,128]{3,2,1,0:T(8,128)(2,1)} %param.7) | copy-start | bytes 6291460
  7.2 18.1 %copy-start.11 = (bf16[3,3,128,128]{3,2,1,0:T(8,128)(2,1)S(1)}, bf16[3,3,128,128]{3,2,1,0:T(8,128)(2,1)}, u32[]{:S(2)}) copy-start(bf16[3,3,128,128]{3,2,1,0:T(8,128)(2,1)} %param.8) | copy-start | bytes 884740
  7.2 16.5 %copy-start.27 = (bf16[256]{0:T(256)(128)(2,1)S(1)}, bf16[256]{0:T(256)(128)(2,1)}, u32[]{:S(2)}) copy-start(bf16[256]{0:T(256)(128)(2,1)} %param.12) | copy-start | bytes 1540
  9.3 16.8 %collective-permute-start.1 = (bf16[8,1,128,128]{3,2,1,0:T(8,128)(2,1)}, bf16[8,1,128,128]{3,2,1,0:T(8,128)(2,1)S(1)}, u32[]{:S(2)}, u32[]{:S(2)}) collective-permute-start(bf16[8,1,128,128]{3,2,1,0:T(8,128)(2,1)} %get-tuple-element.30), channel_id=1, source_target_pairs={{0,1},{1,2},{2,3},{3,4},{4,5},{5,6},{6,7},{8,9},{9,10},{10,11},{11... | collective-permute-start | bytes 786440 | tf_op jit(solution)/shard_map/ppermute | solution.py:19
  13.8 12.3 %collective-permute-start.2 = (bf16[8,1,128,128]{3,2,1,0:T(8,128)(2,1)}, bf16[8,1,128,128]{3,2,1,0:T(8,128)(2,1)S(1)}, u32[]{:S(2)}, u32[]{:S(2)}) collective-permute-start(bf16[8,1,128,128]{3,2,1,0:T(8,128)(2,1)} %get-tuple-element.29), channel_id=1, source_target_pairs={{1,0},{2,1},{3,2},{4,3},{5,4},{6,5},{7,6},{9,8},{10,9},{11,10},{12... | collective-permute-start | bytes 786440 | tf_op jit(solution)/shard_map/ppermute | solution.py:21
  17.6 67.7 %collective-permute-start = (bf16[2,8,128,128]{3,2,1,0:T(8,128)(2,1)}, bf16[2,8,128,128]{3,2,1,0:T(8,128)(2,1)S(1)}, u32[]{:S(2)}, u32[]{:S(2)}) collective-permute-start(bf16[2,8,128,128]{3,2,1,0:T(8,128)(2,1)} %slice.132), channel_id=1, source_target_pairs={{8,0},{16,8},{24,16},{32,24},{40,32},{48,40},{56,48},{64,56},{72,6... | collective-permute-start | bytes 1572872 | tf_op jit(solution)/shard_map/ppermute | solution.py:31
  36.8 8.6 %copy-start.13 = (bf16[1,3,128,128]{3,2,1,0:T(8,128)(2,1)S(1)}, bf16[1,3,128,128]{3,2,1,0:T(8,128)(2,1)}, u32[]{:S(2)}) copy-start(bf16[1,3,128,128]{3,2,1,0:T(8,128)(2,1)} %get-tuple-element.42) | copy-start | bytes 294916
  60.6 8.7 %copy-start.12 = (bf16[1,3,128,128]{3,2,1,0:T(8,128)(2,1)S(1)}, bf16[1,3,128,128]{3,2,1,0:T(8,128)(2,1)}, u32[]{:S(2)}) copy-start(bf16[1,3,128,128]{3,2,1,0:T(8,128)(2,1)} %get-tuple-element.41) | copy-start | bytes 294916
  60.6 14.7 %slice-start.6 = ((s8[6291456]{0:T(1024)(128)(4,1)}), s8[2097152]{0:T(1024)(128)(4,1)S(1)}, s32[]{:S(2)}) async-start(s8[6291456]{0:T(1024)(128)(4,1)} %bitcast.155), calls=%async_computation.8 | async-start | bytes 4194304
  69.3 6.0 %slice-start.7 = ((s8[6291456]{0:T(1024)(128)(4,1)}), s8[4194304]{0:T(1024)(128)(4,1)S(1)}, s32[]{:S(2)}) async-start(s8[6291456]{0:T(1024)(128)(4,1)} %bitcast.155), calls=%async_computation.9 | async-start | bytes 8388608
  69.3 6.0 %copy-start.20 = (bf16[1,3,128,128]{3,2,1,0:T(8,128)(2,1)S(1)}, bf16[1,3,128,128]{3,2,1,0:T(8,128)(2,1)}, u32[]{:S(2)}) copy-start(bf16[1,3,128,128]{3,2,1,0:T(8,128)(2,1)} %get-tuple-element.40) | copy-start | bytes 294916
  75.3 10.0 %copy-start.4 = (bf16[10,8,128,128]{3,2,1,0:T(8,128)(2,1)S(1)}, bf16[10,8,128,128]{3,2,1,0:T(8,128)(2,1)}, u32[]{:S(2)}) copy-start(bf16[10,8,128,128]{3,2,1,0:T(8,128)(2,1)} %constant_dynamic-update-slice_fusion.1) | copy-start | bytes 7864324
  79.4 7.4 %copy-start.7 = (bf16[8192,128]{1,0:T(8,128)(2,1)}, bf16[8192,128]{1,0:T(8,128)(2,1)S(1)}, u32[]{:S(2)}) copy-start(bf16[8192,128]{1,0:T(8,128)(2,1)S(1)} %get-tuple-element.43) | copy-start | bytes 6291460
  80.3 29.7 %collective-permute-start.5 = (bf16[2,8,128,128]{3,2,1,0:T(8,128)(2,1)}, bf16[2,8,128,128]{3,2,1,0:T(8,128)(2,1)}, u32[]{:S(2)}, u32[]{:S(2)}) collective-permute-start(bf16[2,8,128,128]{3,2,1,0:T(8,128)(2,1)} %bitcast.44), channel_id=1, source_target_pairs={{0,8},{8,16},{16,24},{24,32},{32,40},{40,48},{48,56},{56,64},{64,7... | collective-permute-start | bytes 1572872 | tf_op jit(solution)/shard_map/ppermute | solution.py:31
  86.9 10.7 %slice-start.2 = ((s8[6291456]{0:T(1024)(128)(4,1)}), s8[2097152]{0:T(1024)(128)(4,1)S(1)}, s32[]{:S(2)}) async-start(s8[6291456]{0:T(1024)(128)(4,1)} %bitcast.148), calls=%async_computation.4 | async-start | bytes 4194304
  86.9 12.5 %slice-start.4 = ((s8[6291456]{0:T(1024)(128)(4,1)}), s8[4194304]{0:T(1024)(128)(4,1)S(1)}, s32[]{:S(2)}) async-start(s8[6291456]{0:T(1024)(128)(4,1)} %bitcast.151), calls=%async_computation.6 | async-start | bytes 8388608
  91.1 6.5 %slice-start.3 = ((s8[6291456]{0:T(1024)(128)(4,1)}), s8[4194304]{0:T(1024)(128)(4,1)S(1)}, s32[]{:S(2)}) async-start(s8[6291456]{0:T(1024)(128)(4,1)} %bitcast.148), calls=%async_computation.5 | async-start | bytes 8388608
  91.1 8.4 %slice-start.5 = ((s8[6291456]{0:T(1024)(128)(4,1)}), s8[2097152]{0:T(1024)(128)(4,1)S(1)}, s32[]{:S(2)}) async-start(s8[6291456]{0:T(1024)(128)(4,1)} %bitcast.151), calls=%async_computation.7 | async-start | bytes 4194304
  97.6 9.7 %slice-start = ((s8[6291456]{0:T(1024)(128)(4,1)}), s8[4194304]{0:T(1024)(128)(4,1)S(1)}, s32[]{:S(2)}) async-start(s8[6291456]{0:T(1024)(128)(4,1)} %bitcast.145), calls=%async_computation.2 | async-start | bytes 8388608
  99.5 7.8 %slice-start.1 = ((s8[6291456]{0:T(1024)(128)(4,1)}), s8[2097152]{0:T(1024)(128)(4,1)S(1)}, s32[]{:S(2)}) async-start(s8[6291456]{0:T(1024)(128)(4,1)} %bitcast.145), calls=%async_computation.3 | async-start | bytes 4194304
  101.3 30.4 %collective-permute-start.3 = (bf16[8,1,128,128]{3,2,1,0:T(8,128)(2,1)S(1)}, bf16[8,1,128,128]{3,2,1,0:T(8,128)(2,1)S(1)}, u32[]{:S(2)}, u32[]{:S(2)}) collective-permute-start(bf16[8,1,128,128]{3,2,1,0:T(8,128)(2,1)S(1)} %get-tuple-element.24), channel_id=1, source_target_pairs={{0,1},{1,2},{2,3},{3,4},{4,5},{5,6},{6,7},{8,9},{9,10},{10,11},{11... | collective-permute-start | bytes 786440 | tf_op jit(solution)/shard_map/ppermute | solution.py:19
  105.3 26.4 %collective-permute-start.4 = (bf16[8,1,128,128]{3,2,1,0:T(8,128)(2,1)S(1)}, bf16[8,1,128,128]{3,2,1,0:T(8,128)(2,1)S(1)}, u32[]{:S(2)}, u32[]{:S(2)}) collective-permute-start(bf16[8,1,128,128]{3,2,1,0:T(8,128)(2,1)S(1)} %get-tuple-element.25), channel_id=1, source_target_pairs={{1,0},{2,1},{3,2},{4,3},{5,4},{6,5},{7,6},{9,8},{10,9},{11,10},{12... | collective-permute-start | bytes 786440 | tf_op jit(solution)/shard_map/ppermute | solution.py:21
  118.2 35.2 %all-to-all-start = ((bf16[8,1,8,3,128]{4,2,3,1,0:T(8,128)(2,1)}), bf16[8,1,8,3,128]{4,2,3,1,0:T(8,128)(2,1)S(1)}, u32[]{:S(2)}, u32[]{:S(2)}) async-start(bf16[8,1,8,3,128]{4,2,3,1,0:T(8,128)(2,1)} %copy.27), calls=%async_computation | async-start | bytes 98304 | tf_op jit(solution)/shard_map/all_to_all | solution.py:76
  123.2 168.4 %all-reduce.5.cloned.1.call-start = ((), (), s32[]{:S(2)}) async-start(), calls=%async_computation.1 | async-start | bytes 1572864 | tf_op jit(solution)/shard_map/psum | solution.py:115
  131.7 6.8 %slice-start.8 = ((s8[6291456]{0:T(1024)(128)(4,1)}), s8[4194304]{0:T(1024)(128)(4,1)S(1)}, s32[]{:S(2)}) async-start(s8[6291456]{0:T(1024)(128)(4,1)} %bitcast.158), calls=%async_computation.10 | async-start | bytes 8388608
  133.0 5.6 %copy-start.2 = (bf16[8,8,128,128]{3,2,1,0:T(8,128)(2,1)S(1)}, bf16[8,8,128,128]{3,2,1,0:T(8,128)(2,1)}, u32[]{:S(2)}) copy-start(bf16[8,8,128,128]{3,2,1,0:T(8,128)(2,1)} %param.13) | copy-start | bytes 6291460
  133.0 5.6 %slice-start.9 = ((s8[6291456]{0:T(1024)(128)(4,1)}), s8[2097152]{0:T(1024)(128)(4,1)S(1)}, s32[]{:S(2)}) async-start(s8[6291456]{0:T(1024)(128)(4,1)} %bitcast.158), calls=%async_computation.11 | async-start | bytes 4194304
  141.1 4.9 %copy-start.3 = (bf16[8,8,128,128]{3,2,1,0:T(8,128)(2,1)S(1)}, bf16[8,8,128,128]{3,2,1,0:T(8,128)(2,1)}, u32[]{:S(2)}) copy-start(bf16[8,8,128,128]{3,2,1,0:T(8,128)(2,1)} %param.13) | copy-start | bytes 6291460
  141.1 4.9 %copy-start.17 = (bf16[128,128]{0,1:T(8,128)(2,1)S(1)}, bf16[128,128]{0,1:T(8,128)(2,1)}, u32[]{:S(2)}) copy-start(bf16[128,128]{0,1:T(8,128)(2,1)} %get-tuple-element.35) | copy-start | bytes 98308
  141.1 4.9 %copy-start.18 = (bf16[128,128]{0,1:T(8,128)(2,1)S(1)}, bf16[128,128]{0,1:T(8,128)(2,1)}, u32[]{:S(2)}) copy-start(bf16[128,128]{0,1:T(8,128)(2,1)} %get-tuple-element.36) | copy-start | bytes 98308
  141.1 4.9 %copy-start.19 = (bf16[128,128]{0,1:T(8,128)(2,1)S(1)}, bf16[128,128]{0,1:T(8,128)(2,1)}, u32[]{:S(2)}) copy-start(bf16[128,128]{0,1:T(8,128)(2,1)} %get-tuple-element.37) | copy-start | bytes 98308
  (14 other events, 33.7 us)
Sparse Core Ops, SparseCore 0:
  141.2 150.3 all-reduce.4
where the time goes:
time: 303 us; the launch traced here: 302 us
  waiting for transfers between devices  133 us (44%)
  local copies, waits for them, and re-layouts  59.9 us (20%)
  matrix products  40.9 us (13%)
  other arithmetic  28.6 us (9%)
  starting transfers between devices  23.5 us (8%)
  between operations  16 us (5%)
    psum x1, waiting for transfers between devices, shards(): time_sum, space_sum = lax.psum((time_term, space_term), ('tm', 'rows'))  133 us
    reshape x3, local copies, waits for them, and re-layouts, column_stack(): return joined.reshape(-1, joined.shape[-1])  25.9 us
    dot_general x1, local copies, waits for them, and re-layouts, shards(): lax.dot_general(lagged, flat_grad, contract, preferred_element_type=jnp.f...  8.57 us
    ppermute x2, starting transfers between devices, extended(): lax.ppermute(tail, axis, [(i, (i + 1) % count) for i in range(ends)])  8.5 us
    dot_general x3, matrix products, shards(): total = total + jnp.dot(joined, kernel, preferred_element_type=jnp.float32)  6.95 us
    concatenate x1, other arithmetic, column_stack(): joined = jnp.concatenate(parts, axis=-1)  6.67 us
    dot_general x1, matrix products, shards(): pre_act = jnp.dot(stacks[0], space_w[0], preferred_element_type=jnp.float32)  6.54 us
    dot_general x1, matrix products, shards(): jnp.dot(leading, time_back, preferred_element_type=jnp.float32)  6.51 us
  transfers between devices with their start and end apart: 8, of which 1 were waited for; matrix products, arithmetic and copies ran while one was open for 41% of the time, Pallas kernels for 0%

commit v1 on v0

v1 whole, which is shorter than its diff:
```python
import functools
import math

import jax
import jax.numpy as jnp
from jax import lax
from jax.experimental import pallas as pl
from jax.experimental.pallas import tpu as pltpu
from jax.sharding import PartitionSpec as P

PATCH = 8
C = 128
MESH = pl.DeviceIdType.MESH
F32 = jnp.float32
BF16 = jnp.bfloat16


def mm(a, b):
    return jnp.dot(a, b, preferred_element_type=F32)


def mm_nt(a, b):
    return lax.dot_general(a, b, (((1,), (1,)), ((), ())), preferred_element_type=F32)


def shifted(cells, col, step):
    size = cells.shape[0]
    moved = pltpu.roll(cells, (size - step) % size, 0)
    return jnp.where(col == (0 if step < 0 else 127), 0.0, moved)


def kernel(
    nt, nr,
    video, w_space, w_time, w_pixel, w_patch, w_logit, grad,
    out_ig, out_ar, out_lg,
    vpad, gpad, hid, bpad, bcat, vtr, bh, og,
    wf, wb, wt, wp, wpf, wv, stage,
    yb, hsend, hrecv, stat, lgs, pix,
    acc, buf1, s1, buf2, buf3, ob,
    lsem, osem,
    vs, vr, gs, gr, bs, br, hs, hr, ss, sr, ls, lr,
    s1s, s1r, s2s, s2r, s3s, s3r, s4s, s4r, s5s, s5r,
):
    t = lax.axis_index("tm")
    r = lax.axis_index("rows")
    core = lax.rem(r, 2)
    xpos = r // 2
    nx = nr // 2
    partner = r + 1 - 2 * core
    fd, rd, width, _ = video.shape

    def remote(src, dst, ssem, rsem, tt, rr):
        return pltpu.make_async_remote_copy(
            src_ref=src, dst_ref=dst, send_sem=ssem, recv_sem=rsem,
            device_id=(tt, rr), device_id_type=MESH,
        )

    barrier = pltpu.get_barrier_semaphore()
    for d in range(1, nr):
        pl.semaphore_signal(barrier, inc=1, device_id=(t, lax.rem(r + d, nr)), device_id_type=MESH)
    for d in range(1, nt):
        pl.semaphore_signal(barrier, inc=1, device_id=(lax.rem(t + d, nt), r), device_id_type=MESH)

    load_v = pltpu.make_async_copy(video, vpad.at[:, 1 : rd + 1], lsem.at[0])
    load_g = pltpu.make_async_copy(grad, gpad.at[0:fd], lsem.at[1])
    load_v.start()
    load_g.start()

    pl.semaphore_wait(barrier, nr - 1 + nt - 1)

    to_up = remote(video.at[:, 0], vpad.at[:, rd + 1], vs.at[0], vr.at[0], t, jnp.maximum(r - 1, 0))
    to_down = remote(video.at[:, rd - 1], vpad.at[:, 0], vs.at[1], vr.at[1], t, jnp.minimum(r + 1, nr - 1))
    to_prev = remote(grad.at[0:2], gpad.at[fd : fd + 2], gs.at[0], gr.at[0], jnp.maximum(t - 1, 0), r)

    @pl.when(r > 0)
    def _():
        to_up.start()

    @pl.when(r < nr - 1)
    def _():
        to_down.start()

    @pl.when(t > 0)
    def _():
        to_prev.start()

    @pl.when(r == 0)
    def _():
        vpad[:, 0] = jnp.zeros((fd, width, C), BF16)
        bpad[:, 0] = jnp.zeros((fd, width, C), BF16)

    @pl.when(r == nr - 1)
    def _():
        vpad[:, rd + 1] = jnp.zeros((fd, width, C), BF16)
        bpad[:, rd + 1] = jnp.zeros((fd, width, C), BF16)

    @pl.when(t == nt - 1)
    def _():
        gpad[fd : fd + 2] = jnp.zeros((2, rd, width, C), BF16)

    @pl.when(t == 0)
    def _():
        hrecv[...] = jnp.zeros((width, C), F32)

    blank = jnp.zeros((C, C), BF16)
    for dj in range(3):
        for a in range(4):
            for o in range(2):
                rows_at = slice(a * C, (a + 1) * C)
                cols_at = slice(o * C, (o + 1) * C)
                wf[dj, rows_at, cols_at] = w_space[a - o, dj] if 0 <= a - o <= 2 else blank
                di = o + 2 - a
                wb[dj, rows_at, cols_at] = w_space[di, dj].T if 0 <= di <= 2 else blank
    for a in range(4):
        for o in range(2):
            wt[a * C : (a + 1) * C, o * C : (o + 1) * C] = (
                w_time[a - o].T if 0 <= a - o <= 2 else blank
            )

    stage[...] = jnp.zeros((4, C, C), F32)
    pixel_rows = w_pixel[...].astype(F32)
    for g in range(4):
        stage[g, 24 * g : 24 * g + 3, :] = pixel_rows
    eye = (
        lax.broadcasted_iota(jnp.int32, (C, C), 0) == lax.broadcasted_iota(jnp.int32, (C, C), 1)
    ).astype(BF16)
    a_video = mm_nt(eye, stage[0].astype(BF16))
    a_hid = mm_nt(w_time[0], stage[1].astype(BF16))
    a_hid = a_hid + mm_nt(w_time[1], stage[2].astype(BF16))
    a_hid = a_hid + mm_nt(w_time[2], stage[3].astype(BF16))
    high = a_hid.astype(BF16).astype(F32)
    low = a_hid - high
    for u in range(PATCH):
        turn = (lambda m: m) if u == 0 else (lambda m: pltpu.roll(m, 3 * u, 1))
        wp[u, 0:C, 0:C] = turn(a_video).astype(BF16)
        wp[u, 0:C, C : 2 * C] = blank
        wp[u, C : 2 * C, 0:C] = turn(high).astype(BF16)
        wp[u, C : 2 * C, C : 2 * C] = turn(low).astype(BF16)
    for h in range(2):
        wpf[h] = w_patch[:, h * C : (h + 1) * C].astype(F32)
    for v in range(PATCH):
        taps = [wpf[h, pl.ds(v, 24, stride=PATCH), :] for h in range(2)]
        taps = jnp.concatenate(taps, axis=1)
        full = jnp.concatenate([taps, jnp.zeros((C - 24, 2 * C), F32)], axis=0)
        wv[v] = full.astype(BF16)

    acc[...] = jnp.zeros((12, C, C), F32)

    load_v.wait()
    load_g.wait()

    @pl.when(r > 0)
    def _():
        to_up.wait_send()
        to_down.wait_recv()

    @pl.when(r < nr - 1)
    def _():
        to_down.wait_send()
        to_up.wait_recv()

    col512 = lax.rem(lax.broadcasted_iota(jnp.int32, (512, 2 * C), 0), 128)
    col128 = lax.broadcasted_iota(jnp.int32, (128, C), 0)

    def conv(src, f, w, steps):
        lhs = jnp.concatenate(
            [
                jnp.concatenate([src[f, 2 * p + a] for p in range(4)], axis=0)
                for a in range(4)
            ],
            axis=1,
        )
        total = mm(lhs, w[1])
        total = total + shifted(mm(lhs, w[0]), col512, steps[0])
        return total + shifted(mm(lhs, w[2]), col512, steps[1])

    def edge_up(f):
        return remote(bpad.at[f, 1], bpad.at[f, rd + 1], bs.at[f, 0], br.at[f, 0], t, jnp.maximum(r - 1, 0))

    def edge_down(f):
        return remote(bpad.at[f, rd], bpad.at[f, 0], bs.at[f, 1], br.at[f, 1], t, jnp.minimum(r + 1, nr - 1))

    def pair(p, carry):
        f0 = 2 * p

        @pl.when(p == fd // 2 - 1)
        def _():
            @pl.when(t > 0)
            def _():
                to_prev.wait_send()

            @pl.when(t < nt - 1)
            def _():
                to_prev.wait_recv()

        lhs = jnp.concatenate([gpad[f0 + a].reshape(rd * width, C) for a in range(4)], axis=1)
        both = mm(lhs, wt[...])
        bh[0] = both[:, 0:C]
        bh[1] = both[:, C : 2 * C]
        for o in range(2):
            f = f0 + o
            pre = conv(vpad, f, wf, (-1, 1))
            for i in range(rd):
                x = pre[(i // 2) * 128 : (i // 2) * 128 + 128, (i % 2) * C : (i % 2) * C + C]
                s = 0.5 * jnp.tanh(0.5 * x) + 0.5
                h = x * s
                hid[f, i] = h.astype(BF16)
                b = bh[o, i * 128 : (i + 1) * 128, :] * (s + h * (1.0 - s))
                bb = b.astype(BF16)
                bpad[f, i + 1] = bb
                cells = slice(i * 128, (i + 1) * 128)
                bcat[o, cells, C : 2 * C] = bb
                bcat[o, cells, 0:C] = shifted(b, col128, 1).astype(BF16)
                bcat[o, cells, 2 * C : 3 * C] = shifted(b, col128, -1).astype(BF16)

            @pl.when(r > 0)
            def _():
                edge_up(f).start()

            @pl.when(r < nr - 1)
            def _():
                edge_down(f).start()

            for i in range(rd + 2):
                vtr[i * C : (i + 1) * C, :] = vpad[f, i].T
            lead = jnp.concatenate([gpad[f + k].reshape(rd * width, C) for k in range(3)], axis=1)
            turned = jnp.concatenate([hid[f, i].T for i in range(rd)], axis=1)
            tg = mm(turned, lead)
            for k in range(3):
                acc[9 + k] += tg[:, k * C : (k + 1) * C]
            rows_t = jnp.concatenate([vtr[i * C : (i + 3) * C, :] for i in range(rd)], axis=1)
            sg = mm(rows_t, bcat[o])
            for di in range(3):
                for dj in range(3):
                    acc[di * 3 + dj] += sg[di * C : (di + 1) * C, dj * C : (dj + 1) * C]
        return carry

    lax.fori_loop(0, fd // 2, pair, 0)

    def step1():
        return remote(
            acc.at[pl.ds(6 * (1 - core), 6)], buf1, s1s.at[0], s1r.at[0], t, partner
        )

    step1().start()

    y = None
    for u in range(PATCH):
        lhs = jnp.concatenate(
            [vpad[:, u + 1].reshape(fd * width, C), hid[:, u].reshape(fd * width, C)], axis=1
        )
        term = mm(lhs, wp[u])
        y = term if y is None else y + term
    yb[...] = (y[:, 0:C] + y[:, C : 2 * C]).reshape(fd, width, C)
    lane = lax.broadcasted_iota(jnp.int32, (width, C), 1)

    def group(m, g):
        return m if g == 0 else pltpu.roll(m, C - 24 * g, 1)

    first = group(yb[fd - 1], 2) + group(yb[fd - 2], 3)
    second = pltpu.roll(yb[fd - 1], 128 - 48, 1)
    hsend[...] = jnp.where(lane < 24, first, jnp.where(lane < 48, second, 0.0))
    halo = remote(hsend, hrecv, hs.at[0], hr.at[0], jnp.where(t < nt - 1, t + 1, t - 1), r)

    @pl.when(t < nt - 1)
    def _():
        halo.start()

    step1().wait()
    piece = 768 // nt
    half = acc[pl.ds(6 * core, 6)] + buf1[...]
    s1[...] = half.reshape(nt, piece, C)

    def step2(d):
        peer = lax.rem(t + d, nt)
        return remote(s1.at[peer], buf2.at[t], s2s.at[d], s2r.at[t], peer, r)

    def step2_in(d):
        peer = lax.rem(t + d, nt)
        return remote(s1.at[t], buf2.at[peer], s2s.at[d], s2r.at[peer], peer, r)

    for d in range(1, nt):
        step2(d).start()
    buf2[t] = s1[t]

    def finish_frame(f):
        @pl.when(r > 0)
        def _():
            edge_up(f).wait_send()
            edge_down(f).wait_recv()

        @pl.when(r < nr - 1)
        def _():
            edge_down(f).wait_send()
            edge_up(f).wait_recv()

        out = conv(bpad, f, wb, (1, -1))
        for i in range(rd):
            part = out[(i // 2) * 128 : (i // 2) * 128 + 128, (i % 2) * C : (i % 2) * C + C]
            og[f, i] = (gpad[f, i].astype(F32) + part).astype(BF16)
        pltpu.make_async_copy(og.at[f], out_ig.at[f], osem.at[f]).start()

    def frames(lo, hi):
        lax.fori_loop(lo, hi, lambda f, c: (finish_frame(f), c)[1], 0)

    frames(0, 3)

    @pl.when(t > 0)
    def _():
        halo.wait_recv()

    @pl.when(t < nt - 1)
    def _():
        halo.wait_send()

    lane8 = lax.broadcasted_iota(jnp.int32, (8, C), 1)
    sub8 = lax.broadcasted_iota(jnp.int32, (8, C), 0)
    count = 24.0 * width
    stats = jnp.zeros((8, C), F32)
    for f in range(fd):
        m = yb[f] + group(yb[f], 1)
        m = m + (group(yb[f - 1], 2) if f >= 1 else 0.0)
        m = m + (group(yb[f - 2], 3) if f >= 2 else 0.0)
        if f < 2:
            m = m + group(hrecv[...], f)
        m = jnp.where(lane < 24, m, 0.0).astype(BF16).astype(F32)
        pix[f * width : (f + 1) * width, :] = m
        mean = jnp.sum(m, keepdims=True) / count
        away = jnp.where(lane < 24, m - mean, 0.0)
        square = jnp.sum(away * away, keepdims=True)
        here = jnp.where(lane8 == 0, mean, jnp.where(lane8 == 1, square, 0.0))
        stats = stats + jnp.where(sub8 == f, here, 0.0)
    stat[r] = stats

    def stat_out(d):
        return remote(stat.at[r], stat.at[r], ss.at[d], sr.at[r], t, lax.rem(r + d, nr))

    def stat_in(d):
        peer = lax.rem(r + d, nr)
        return remote(stat.at[r], stat.at[peer], ss.at[d], sr.at[peer], t, peer)

    for d in range(1, nr):
        stat_out(d).start()

    frames(3, 5)

    for d in range(1, nt):
        step2(d).wait_send()
        step2_in(d).wait_recv()
    buf3[xpos] = jnp.sum(buf2[...], axis=0)

    def step3(d):
        return remote(
            buf3.at[xpos], buf3.at[xpos], s3s.at[d], s3r.at[xpos], t,
            2 * lax.rem(xpos + d, nx) + core,
        )

    def step3_in(d):
        peer = lax.rem(xpos + d, nx)
        return remote(
            buf3.at[xpos], buf3.at[peer], s3s.at[d], s3r.at[peer], t, 2 * peer + core
        )

    for d in range(1, nx):
        step3(d).start()

    for d in range(1, nr):
        stat_out(d).wait_send()
        stat_in(d).wait_recv()

    every = stat[...]
    means = jnp.sum(jnp.where(lane8 == 0, every, 0.0), axis=2, keepdims=True)
    squares = jnp.sum(jnp.where(lane8 == 1, every, 0.0), axis=2, keepdims=True)
    center = jnp.sum(means, axis=0, keepdims=True) / nr
    apart = means - center
    spread = jnp.sum(squares + count * apart * apart, axis=0, keepdims=True) / (count * nr)
    scale = lax.rsqrt(spread + 1e-05)
    for f in range(fd):
        m = pix[f * width : (f + 1) * width, :]
        m = (m - center[0, f : f + 1, :]) * scale[0, f : f + 1, :]
        pix[f * width : (f + 1) * width, :] = m
    inner = jnp.zeros((fd * width // PATCH, 2 * C), F32)
    for v in range(PATCH):
        taken = pix[pl.ds(v, fd * width // PATCH, stride=PATCH), :]
        inner = inner + mm(taken.astype(BF16), wv[v])
    inner = jnp.where(inner >= 0, inner, 0.2 * inner)
    in_high = inner.astype(BF16)
    in_low = (inner - in_high.astype(F32)).astype(BF16)
    wl = jnp.broadcast_to(w_logit[...], (8, 2 * C)).astype(BF16)
    lgs[r] = mm_nt(wl, in_high) + mm_nt(wl, in_low)

    def lg_out(d):
        return remote(lgs.at[r], lgs.at[r], ls.at[d], lr.at[r], t, lax.rem(r + d, nr))

    def lg_in(d):
        peer = lax.rem(r + d, nr)
        return remote(lgs.at[r], lgs.at[peer], ls.at[d], lr.at[peer], t, peer)

    for d in range(1, nr):
        lg_out(d).start()

    for d in range(1, nx):
        step3(d).wait_send()
        step3_in(d).wait_recv()
    ob[core, t] = jnp.sum(buf3[...], axis=0)

    def step4(d):
        return remote(ob.at[core, t], ob.at[core, t], s4s.at[d], s4r.at[t], lax.rem(t + d, nt), r)

    def step4_in(d):
        peer = lax.rem(t + d, nt)
        return remote(ob.at[core, t], ob.at[core, peer], s4s.at[d], s4r.at[peer], peer, r)

    for d in range(1, nt):
        step4(d).start()

    frames(5, 8)

    for d in range(1, nt):
        step4(d).wait_send()
        step4_in(d).wait_recv()
    step5 = remote(ob.at[core], ob.at[core], s5s.at[0], s5r.at[0], t, partner)
    step5_in = remote(ob.at[core], ob.at[1 - core], s5s.at[0], s5r.at[0], t, partner)
    step5.start()

    for d in range(1, nr):
        lg_out(d).wait_send()
        lg_in(d).wait_recv()
    table = jnp.concatenate([lgs[i, 0:1, :] for i in range(nr)], axis=0)
    out_lg[...] = pltpu.roll(table, lax.rem(C - 16 * r, C), 1)

    step5.wait_send()
    step5_in.wait_recv()
    out_ar[...] = ob[...]
    for f in range(fd):
        pltpu.make_async_copy(og.at[f], out_ig.at[f], osem.at[f]).wait()


def shards(video, w_space, w_time, w_pixel, w_patch, w_logit, grad_out):
    fd, rd, width, chans = video.shape
    nt = lax.axis_size("tm")
    nr = lax.axis_size("rows")
    hbm = pl.BlockSpec(memory_space=pl.ANY)
    vmem = pl.BlockSpec(memory_space=pltpu.VMEM)
    dma = pltpu.SemaphoreType.DMA
    piece = 768 // nt
    scratch = [
        pltpu.VMEM((fd, rd + 2, width, chans), BF16),
        pltpu.VMEM((fd + 2, rd, width, chans), BF16),
        pltpu.VMEM((fd, rd, width, chans), BF16),
        pltpu.VMEM((fd, rd + 2, width, chans), BF16),
        pltpu.VMEM((2, rd * width, 3 * chans), BF16),
        pltpu.VMEM(((rd + 2) * chans, width), BF16),
        pltpu.VMEM((2, rd * width, chans), F32),
        pltpu.VMEM((fd, rd, width, chans), BF16),
        pltpu.VMEM((3, 4 * chans, 2 * chans), BF16),
        pltpu.VMEM((3, 4 * chans, 2 * chans), BF16),
        pltpu.VMEM((4 * chans, 2 * chans), BF16),
        pltpu.VMEM((PATCH, 2 * chans, 2 * chans), BF16),
        pltpu.VMEM((2, 192, chans), F32),
        pltpu.VMEM((PATCH, chans, 2 * chans), BF16),
        pltpu.VMEM((4, chans, chans), F32),
        pltpu.VMEM((fd, width, chans), F32),
        pltpu.VMEM((width, chans), F32),
        pltpu.VMEM((width, chans), F32),
        pltpu.VMEM((nr, 8, chans), F32),
        pltpu.VMEM((nr, 8, chans), F32),
        pltpu.VMEM((fd * width, chans), F32),
        pltpu.VMEM((12, chans, chans), F32),
        pltpu.VMEM((6, chans, chans), F32),
        pltpu.VMEM((nt, piece, chans), F32),
        pltpu.VMEM((nt, piece, chans), F32),
        pltpu.VMEM((nr // 2, piece, chans), F32),
        pltpu.VMEM((2, nt, piece, chans), F32),
        dma((2,)), dma((fd,)),
        dma((2,)), dma((2,)), dma((1,)), dma((1,)), dma((fd, 2)), dma((fd, 2)),
        dma((1,)), dma((1,)), dma((nr,)), dma((nr,)), dma((nr,)), dma((nr,)),
        dma((1,)), dma((1,)), dma((nt,)), dma((nt,)), dma((nr // 2,)), dma((nr // 2,)),
        dma((nt,)), dma((nt,)), dma((1,)), dma((1,)),
    ]
    ig, ar, lg = pl.pallas_call(
        functools.partial(kernel, nt, nr),
        out_shape=(
            jax.ShapeDtypeStruct(video.shape, BF16),
            jax.ShapeDtypeStruct((2, nt, piece, chans), F32),
            jax.ShapeDtypeStruct((nr, chans), F32),
        ),
        in_specs=[hbm, vmem, vmem, vmem, vmem, vmem, hbm],
        out_specs=(hbm, vmem, vmem),
        scratch_shapes=scratch,
        compiler_params=pltpu.CompilerParams(
            collective_id=0, has_side_effects=True, vmem_limit_bytes=56 * 1024 * 1024
        ),
        cost_estimate=pl.CostEstimate(
            flops=2 * fd * rd * width * chans * chans * 36,
            bytes_accessed=3 * fd * rd * width * chans * 2,
            transcendentals=fd * rd * width * chans,
        ),
        name="block_step",
    )(video, w_space, w_time, w_pixel, w_patch, w_logit.reshape(1, 2 * chans), grad_out)
    sums = ar.reshape(12, chans, chans) * (1.0 / math.sqrt(fd * rd * width * nt * nr))
    logits = lg[:, 0:16].reshape(1, nr, 16)
    return (ig, sums[0:9].reshape(3, 3, chans, chans), sums[9:12], logits)


def solution(mesh):
    in_specs = (P("tm", "rows", None, None), P(), P(), P(), P(), P(), P("tm", "rows", None, None))
    out_specs = (P("tm", "rows", None, None), P(), P(), P(("tm", "rows"), None, None))
    return jax.shard_map(shards, mesh=mesh, in_specs=in_specs, out_specs=out_specs, check_vma=False)
```

time: 303 us -> 61 us (0.20)
  waiting for transfers between devices: 133 us -> 0 us
  local copies, waits for them, and re-layouts: 59.9 us -> 5.52 us
  Pallas kernels: 0 us -> 53.5 us
  matrix products: 40.9 us -> 0 us
  other arithmetic: 28.6 us -> 1.18 us
  starting transfers between devices: 23.5 us -> 0 us
  between operations: 16 us -> 0.65 us
    psum x1 -> x0, waiting for transfers between devices: 133 us -> none  [shards(): time_sum, space_sum = lax.psum((time_term, space_term), ('tm', 'rows'))]
    pallas_call x0 -> x1, Pallas kernels: none -> 53.5 us  [shards(): pl.pallas_call(functools.partial(kernel, nt, nr), out_shape=(jax.ShapeDty...]
    dot_general x14 -> x0, matrix products: 40.9 us -> none  [the longest x3 6.95 us: shards(): total = total + jnp.dot(joined, kernel, preferred_element_type=jnp.float32)]
    reshape x5 -> x2, local copies, waits for them, and re-layouts: 26.8 us -> 2.65 us  [the longest x1 1.43 us: shards(): logits = lg[:, 0:16].reshape(1, nr, 16)]
    concatenate x6 -> x0, other arithmetic: 19.5 us -> none  [the longest x1 6.67 us: column_stack(): joined = jnp.concatenate(parts, axis=-1)]
    ppermute x6 -> x0, starting transfers between devices: 18.6 us -> none  [the longest x2 8.5 us: extended(): lax.ppermute(tail, axis, [(i, (i + 1) % count) for i in range(ends)])]
    slice x8 -> x2, local copies, waits for them, and re-layouts: 15.4 us -> 1.55 us  [shards(): return (ig, sums[0:9].reshape(3, 3, chans, chans), sums[9:12], logits)]
    dot_general x1 -> x0, local copies, waits for them, and re-layouts: 8.57 us -> none  [shards(): lax.dot_general(lagged, flat_grad, contract, preferred_element_type=jnp.f...]
  transfers between devices with their start and end apart: 8 -> 0, of which waited for: 1 -> 0; matrix products, arithmetic and copies ran while one was open for 41% -> 0% of each run, Pallas kernels for 0% -> 0%
where the time goes in v1:
time: 61 us; the launch traced here: 60.8 us
  Pallas kernels  53.5 us (88%)
  local copies, waits for them, and re-layouts  5.52 us (9%)
  other arithmetic  1.18 us (2%)
  between operations  0.65 us (1%)
    pallas_call x1, Pallas kernels, shards(): pl.pallas_call(functools.partial(kernel, nt, nr), out_shape=(jax.ShapeDty...  53.5 us
    slice x2, local copies, waits for them, and re-layouts, shards(): return (ig, sums[0:9].reshape(3, 3, chans, chans), sums[9:12], logits)  1.55 us
    reshape x1, local copies, waits for them, and re-layouts, shards(): logits = lg[:, 0:16].reshape(1, nr, 16)  1.43 us
    unnamed x3, local copies, waits for them, and re-layouts  1.32 us
    reshape x1, local copies, waits for them, and re-layouts, shards(): w_logit.reshape(1, 2 * chans)  1.22 us

profile of v1, /device:TPU:1, one launch (start us, length us, event | category | flops | bytes accessed | tf_op | source)
XLA Modules:
  0.0 60.8 jit_solution(14830658950200547999)
XLA Ops:
  0.6 1.2 %reshape.20.w_logit = bf16[1,256]{1,0:T(2,128)(2,1)} reshape(bf16[256]{0:T(256)(128)(2,1)} %param.12) | data formatting | bytes 1024 | tf_op jit(solution)/shard_map/reshape | solution.py:500
  1.9 53.5 %block_step.1 = (bf16[8,8,128,128]{3,2,1,0:T(8,128)(2,1)}, f32[2,16,48,128]{3,2,1,0:T(8,128)}, f32[8,128]{1,0:T(8,128)}) custom-call(bf16[8,8,128,128]{3,2,1,0:T(8,128)(2,1)} %video.1, bf16[3,3,128,128]{3,2,1,0:T(8,128)(2,1)} %w_space.1, bf16[3,128,128]{2,1,0:T(8,128)(2,1)} %w_time.1, bf16[3,128]{1,0:T(4,128)(2,1)} %w_pixel.1, bf16[192,256]{1,0:T(8,128)(2,1)} %w_patch.1, ...), custom_call_target="tpu_custom_call" | custom-call | flops 9663676416 | bytes 6291456 | tf_op jit(solution)/shard_map/block_step/pallas_call | solution.py:481
  55.3 0.0 copy-start
  55.3 1.4 %slice_bitcast_fusion = f32[1,8,16]{2,1,0:T(8,128)} fusion(f32[8,128]{1,0:T(8,128)} %get-tuple-element.9), kind=kLoop, calls=%fused_computation.1 | loop fusion | bytes 1024 | tf_op jit(solution)/shard_map/reshape | solution.py:502
  56.8 1.2 %broadcast_multiply_fusion = f32[2,16,48,128]{3,2,1,0:T(8,128)S(1)} fusion(f32[2,16,48,128]{3,2,1,0:T(8,128)} %get-tuple-element.8), kind=kLoop, calls=%fused_computation | loop fusion | flops 196608 | bytes 1572864 | tf_op jit(solution)/shard_map/mul | solution.py:501
  58.0 0.7 %slice.13 = f32[3,128,128]{2,1,0:T(8,128)} slice(f32[12,128,128]{2,1,0:T(8,128)S(1)} %bitcast.4), slice={[9:12], [0:128], [0:128]} | slice | bytes 393216 | tf_op jit(solution)/shard_map/slice | solution.py:503
  58.6 0.9 %slice.12 = f32[9,128,128]{2,1,0:T(8,128)} slice(f32[12,128,128]{2,1,0:T(8,128)S(1)} %bitcast.5), slice={[0:9], [0:128], [0:128]} | slice | bytes 1179648 | tf_op jit(solution)/shard_map/slice | solution.py:503
  59.5 0.0 copy-done
  59.5 1.3 %copy.12 = bf16[8,8,128,128]{3,2,1,0:T(8,128)(2,1)} copy(bf16[8,8,128,128]{3,2,1,0:T(8,128)(2,1)S(1)} %copy-done) | data formatting | bytes 4194304
Async XLA Ops:
  55.3 4.2 %copy-start = (bf16[8,8,128,128]{3,2,1,0:T(8,128)(2,1)S(1)}, bf16[8,8,128,128]{3,2,1,0:T(8,128)(2,1)}, u32[]{:S(2)}) copy-start(bf16[8,8,128,128]{3,2,1,0:T(8,128)(2,1)} %get-tuple-element.14) | copy-start | bytes 6291460

commit v2 on v1

v2 whole, which is shorter than its diff:
```python
import functools
import math

import jax
import jax.numpy as jnp
from jax import lax
from jax.experimental import pallas as pl
from jax.experimental.pallas import tpu as pltpu
from jax.sharding import PartitionSpec as P

PATCH = 8
C = 128
LINE = C + 16
MESH = pl.DeviceIdType.MESH
F32 = jnp.float32
BF16 = jnp.bfloat16


def mm(a, b):
    return jnp.dot(a, b, preferred_element_type=F32)


def mm_nt(a, b):
    return lax.dot_general(a, b, (((1,), (1,)), ((), ())), preferred_element_type=F32)


def kernel(
    nt, nr, factor,
    video, w_space_in, w_time_in, w_pixel_in, w_patch_in, w_logit_in, grad,
    out_ig, out_sg, out_tg, out_lg,
    vpad, gpad, hid, bpad, bleft, bright, vtr, htr, bh, og,
    za, zb, line_a, line_b, ya, yb2,
    wf, wb, wt, wp, wpf, wv, stage,
    w_space, w_time, w_pixel, w_patch, w_logit,
    yb, hsend, hrecv, stat, lgs, pix,
    acc, pair, s1, s2, s3, ob,
    lsem, osem, wsem,
    vs, vr, gs, gr, bs, br, hs, hr, ss, sr, ls, lr,
    s1s, s1r, s2s, s2r, s3s, s3r, s4s, s4r, s5s, s5r,
):
    t = lax.axis_index("tm")
    r = lax.axis_index("rows")
    core = lax.rem(r, 2)
    xpos = r // 2
    nx = nr // 2
    partner = r + 1 - 2 * core
    fd, rd, width, _ = video.shape
    above = jnp.maximum(r - 1, 0)
    below = jnp.minimum(r + 1, nr - 1)

    def remote(src, dst, ssem, rsem, tt, rr):
        return pltpu.make_async_remote_copy(
            src_ref=src, dst_ref=dst, send_sem=ssem, recv_sem=rsem,
            device_id=(tt, rr), device_id_type=MESH,
        )

    barrier = pltpu.get_barrier_semaphore()
    for d in range(1, nr):
        pl.semaphore_signal(barrier, inc=1, device_id=(t, lax.rem(r + d, nr)), device_id_type=MESH)
    for d in range(1, nt):
        pl.semaphore_signal(barrier, inc=1, device_id=(lax.rem(t + d, nt), r), device_id_type=MESH)

    weights = ((w_space_in, w_space), (w_time_in, w_time), (w_pixel_in, w_pixel),
               (w_patch_in, w_patch), (w_logit_in, w_logit))
    loads = [pltpu.make_async_copy(a, b, wsem.at[i]) for i, (a, b) in enumerate(weights)]
    for load in loads:
        load.start()
    load_g = pltpu.make_async_copy(grad, gpad.at[0:fd], lsem.at[1])
    load_v = pltpu.make_async_copy(video, vpad.at[:, 1 : rd + 1], lsem.at[0])
    load_g.start()
    load_v.start()

    edge = jnp.zeros((8, C), F32)
    for z in (za, zb, ya, yb2):
        for dj in range(3):
            for q in range(z.shape[1]):
                z[dj, q, 0:8] = edge
                z[dj, q, C + 8 : LINE] = edge
    for z in (line_a, line_b):
        for q in range(4):
            z[q, 0:8] = edge
            z[q, C + 8 : LINE] = edge

    for load in loads:
        load.wait()

    blank = jnp.zeros((C, C), BF16)
    for a in range(4):
        for o in range(2):
            at = (slice(a * C, (a + 1) * C), slice(o * C, (o + 1) * C))
            lag = a - o
            wt[at] = w_time[lag].T * 0.5 if 0 <= lag <= 2 else blank
            for dj in range(3):
                wf[(dj,) + at] = w_space[lag, dj] * 0.5 if 0 <= lag <= 2 else blank

    pl.semaphore_wait(barrier, nr - 1 + nt - 1)

    parts = (pl.ds(0, 3), pl.ds(3, fd - 3))
    to_up = [
        remote(video.at[at, 0], vpad.at[at, rd + 1], vs.at[0, e], vr.at[0, e], t, above)
        for e, at in enumerate(parts)
    ]
    to_down = [
        remote(video.at[at, rd - 1], vpad.at[at, 0], vs.at[1, e], vr.at[1, e], t, below)
        for e, at in enumerate(parts)
    ]
    to_prev = remote(grad.at[0:2], gpad.at[fd : fd + 2], gs.at[0], gr.at[0], jnp.maximum(t - 1, 0), r)

    for e in range(2):
        @pl.when(r > 0)
        def _():
            to_up[e].start()

        @pl.when(r < nr - 1)
        def _():
            to_down[e].start()

    @pl.when(t > 0)
    def _():
        to_prev.start()

    @pl.when(r == 0)
    def _():
        vpad[:, 0] = jnp.zeros((fd, width, C), BF16)
        bpad[:, 0] = jnp.zeros((fd, width, C), BF16)

    @pl.when(r == nr - 1)
    def _():
        vpad[:, rd + 1] = jnp.zeros((fd, width, C), BF16)
        bpad[:, rd + 1] = jnp.zeros((fd, width, C), BF16)

    @pl.when(t == nt - 1)
    def _():
        gpad[fd : fd + 2] = jnp.zeros((2, rd, width, C), BF16)

    @pl.when(t == 0)
    def _():
        hrecv[...] = jnp.zeros((width, C), F32)

    def back_hidden(f0):
        lhs = jnp.concatenate([gpad[f0 + a].reshape(rd * width, C) for a in range(4)], axis=1)
        both = mm(lhs, wt[...])
        bh[f0] = both[:, 0:C]
        bh[f0 + 1] = both[:, C : 2 * C]

    load_g.wait()
    for f0 in range(0, fd - 2, 2):
        back_hidden(f0)

    load_v.wait()

    def taps(src, f, starts, w, z):
        lhs = jnp.concatenate(
            [jnp.concatenate([src[f, 2 * p + a] for p in starts], axis=0) for a in range(4)], axis=1
        )
        for dj in range(3):
            part = mm(lhs, w[dj])
            for k in range(len(starts)):
                for o in range(2):
                    z[dj, 2 * k + o, 8 : C + 8] = part[k * C : (k + 1) * C, o * C : (o + 1) * C]

    def joined(z, q, steps):
        mid = z[1, q, 8 : C + 8]
        return mid + z[0, q, 8 + steps[0] : C + 8 + steps[0]] + z[2, q, 8 + steps[1] : C + 8 + steps[1]]

    groups = ((0, fd - 2), (fd - 2, 2))

    def edge_up(g):
        at = pl.ds(*groups[g])
        return remote(bpad.at[at, 1], bpad.at[at, rd + 1], bs.at[g, 0], br.at[g, 0], t, above)

    def edge_down(g):
        at = pl.ds(*groups[g])
        return remote(bpad.at[at, rd], bpad.at[at, 0], bs.at[g, 1], br.at[g, 1], t, below)

    def send_edges(g):
        @pl.when(r > 0)
        def _():
            edge_up(g).start()

        @pl.when(r < nr - 1)
        def _():
            edge_down(g).start()

    late = fd - 2
    units = 2 * fd

    def place(u):
        last = u // (2 * late)
        f = (1 - last) * lax.rem(u, late) + last * (late + lax.rem(u, 2))
        outer = (1 - last) * (u // late) + last * lax.rem(u // 2, 2)
        return f, outer, (1 - outer, 2 + outer)

    def forward(u, z):
        f, _, starts = place(u)
        taps(vpad, f, starts, wf, z)

    def activate(u, z, line):
        f, outer, starts = place(u)
        for k in range(2):
            for o in range(2):
                q = 2 * k + o
                i = 2 * starts[k] + o
                x = joined(z, q, (-1, 1))
                th = jnp.tanh(x)
                up = 1.0 + th
                h = x * up
                hb = h.astype(BF16)
                hid[f, i] = hb
                htr[f, i] = hb.T
                b = bh[f, pl.ds(i * C, C), :] * (up + h * (1.0 - th))
                line[q, 8 : C + 8] = b
                bpad[f, i + 1] = b.astype(BF16)
                bleft[f, i] = line[q, 9 : C + 9].astype(BF16)
                bright[f, i] = line[q, 7 : C + 7].astype(BF16)
                vtr[f, i + 1] = vpad[f, i + 1].T

        @pl.when(outer == 1)
        def _():
            vtr[f, 0] = vpad[f, 0].T
            vtr[f, rd + 1] = vpad[f, rd + 1].T

    def two_units(k, carry):
        forward(2 * k + 1, zb)
        activate(2 * k, za, line_a)

        for e in range(2):
            @pl.when(k == late // 2 - 1 + e)
            def _():
                @pl.when(r > 0)
                def _():
                    to_up[e].wait_send()
                    to_down[e].wait_recv()

                @pl.when(r < nr - 1)
                def _():
                    to_down[e].wait_send()
                    to_up[e].wait_recv()

        forward(jnp.minimum(2 * k + 2, units - 1), za)
        activate(2 * k + 1, zb, line_b)
        return carry

    mine = pl.ds(6 * core, 6)
    other = pl.ds(6 * (1 - core), 6)

    def sum1():
        return remote(acc.at[other], pair, s1s.at[0], s1r.at[0], t, partner)

    def sum2(d):
        peer = lax.rem(t + d, nt)
        return remote(s1.at[peer], s2.at[t], s2s.at[d], s2r.at[t], peer, r)

    def sum2_in(d):
        peer = lax.rem(t + d, nt)
        return remote(s1.at[t], s2.at[peer], s2s.at[d], s2r.at[peer], peer, r)

    def sum3(d):
        peer = lax.rem(xpos + d, nx)
        return remote(s3.at[xpos], s3.at[xpos], s3s.at[d], s3r.at[xpos], t, 2 * peer + core)

    def sum3_in(d):
        peer = lax.rem(xpos + d, nx)
        return remote(s3.at[xpos], s3.at[peer], s3s.at[d], s3r.at[peer], t, 2 * peer + core)

    def back4(d):
        return remote(
            ob.at[core, t], ob.at[core, t], s4s.at[d], s4r.at[t], lax.rem(t + d, nt), r
        )

    def back4_in(d):
        peer = lax.rem(t + d, nt)
        return remote(ob.at[core, t], ob.at[core, peer], s4s.at[d], s4r.at[peer], peer, r)

    back5 = remote(ob.at[core], ob.at[core], s5s.at[0], s5r.at[0], t, partner)
    back5_in = remote(ob.at[core], ob.at[1 - core], s5s.at[0], s5r.at[0], t, partner)

    def go2():
        sum1().wait()
        s1[...] = (acc[mine] + pair[...]).reshape(s1.shape).astype(s1.dtype)
        for d in range(1, nt):
            sum2(d).start()
        s2[t] = s1[t]

    def go3():
        for d in range(1, nt):
            sum2(d).wait_send()
            sum2_in(d).wait_recv()
        s3[xpos] = jnp.sum(s2[...].astype(F32), axis=0)
        for d in range(1, nx):
            sum3(d).start()

    def go4():
        for d in range(1, nx):
            sum3(d).wait_send()
            sum3_in(d).wait_recv()
        ob[core, t] = (jnp.sum(s3[...], axis=0) * factor).astype(BF16)
        for d in range(1, nt):
            back4(d).start()

    def go5():
        for d in range(1, nt):
            back4(d).wait_send()
            back4_in(d).wait_recv()
        back5.start()

    def finish_sums():
        back5.wait_send()
        back5_in.wait_recv()
        blocks = ob[...].reshape(12, C, C).astype(F32)
        for di in range(3):
            for dj in range(3):
                out_sg[di, dj] = blocks[3 * di + dj]
        for k in range(3):
            out_tg[k] = blocks[9 + k]

    acc[...] = jnp.zeros((12, C, C), F32)

    def cells(x, f):
        return jnp.concatenate([x[f], x[f + 1]], axis=0).reshape(2 * rd * width, C)

    def grads(h, carry):
        f = 2 * h
        lhs = jnp.concatenate(
            [vtr[f + e, i : i + 3].reshape(3 * C, width) for e in range(2) for i in range(rd)], axis=1
        )
        mid = jnp.concatenate([bpad[f + e, 1 : rd + 1] for e in range(2)], axis=0)
        rhs = jnp.concatenate(
            [cells(bleft, f), mid.reshape(2 * rd * width, C), cells(bright, f)], axis=1
        )
        sg = mm(lhs, rhs)
        for di in range(3):
            for dj in range(3):
                acc[3 * di + dj] += sg[di * C : (di + 1) * C, dj * C : (dj + 1) * C]
        lhs = jnp.concatenate([htr[f + e, i] for e in range(2) for i in range(rd)], axis=1)
        tg = mm(lhs, jnp.concatenate([cells(gpad, f + k) for k in range(3)], axis=1))
        for k in range(3):
            acc[9 + k] += tg[:, k * C : (k + 1) * C]
        return carry

    forward(0, za)
    lax.fori_loop(0, late, two_units, 0)
    send_edges(0)
    lax.fori_loop(0, late // 2, grads, 0)

    @pl.when(t > 0)
    def _():
        to_prev.wait_send()

    @pl.when(t < nt - 1)
    def _():
        to_prev.wait_recv()

    back_hidden(late)
    lax.fori_loop(late, units // 2, two_units, 0)
    send_edges(1)
    grads(late // 2, 0)
    sum1().start()

    stage[...] = jnp.zeros((4, C, C), F32)
    pixel_rows = w_pixel[...].astype(F32)
    for g in range(4):
        stage[g, 24 * g : 24 * g + 3, :] = pixel_rows
    eye = (
        lax.broadcasted_iota(jnp.int32, (C, C), 0) == lax.broadcasted_iota(jnp.int32, (C, C), 1)
    ).astype(BF16)
    a_video = mm_nt(eye, stage[0].astype(BF16))
    a_hid = mm_nt(w_time[0], stage[1].astype(BF16))
    a_hid = a_hid + mm_nt(w_time[1], stage[2].astype(BF16))
    a_hid = a_hid + mm_nt(w_time[2], stage[3].astype(BF16))
    high = a_hid.astype(BF16).astype(F32)
    low = a_hid - high
    for u in range(PATCH):
        turn = (lambda m: m) if u == 0 else (lambda m: pltpu.roll(m, 3 * u, 1))
        wp[u, 0:C, 0:C] = turn(a_video).astype(BF16)
        wp[u, 0:C, C : 2 * C] = blank
        wp[u, C : 2 * C, 0:C] = turn(high).astype(BF16)
        wp[u, C : 2 * C, C : 2 * C] = turn(low).astype(BF16)
    y = None
    for u in range(PATCH):
        lhs = jnp.concatenate(
            [vpad[:, u + 1].reshape(fd * width, C), hid[:, u].reshape(fd * width, C)], axis=1
        )
        term = mm(lhs, wp[u])
        y = term if y is None else y + term
    yb[...] = (y[:, 0:C] + y[:, C : 2 * C]).reshape(fd, width, C)
    lane = lax.broadcasted_iota(jnp.int32, (width, C), 1)

    def group(m, g):
        return m if g == 0 else pltpu.roll(m, C - 24 * g, 1)

    first = group(yb[fd - 1], 2) + group(yb[fd - 2], 3)
    second = pltpu.roll(yb[fd - 1], 128 - 48, 1)
    hsend[...] = jnp.where(lane < 24, first, jnp.where(lane < 48, second, 0.0))
    halo = remote(hsend, hrecv, hs.at[0], hr.at[0], jnp.where(t < nt - 1, t + 1, t - 1), r)

    @pl.when(t < nt - 1)
    def _():
        halo.start()

    for a in range(4):
        for o in range(2):
            at = (slice(a * C, (a + 1) * C), slice(o * C, (o + 1) * C))
            di = o + 2 - a
            for dj in range(3):
                wb[(dj,) + at] = w_space[di, dj].T if 0 <= di <= 2 else blank

    def arrived(g):
        @pl.when(r > 0)
        def _():
            edge_up(g).wait_send()
            edge_down(g).wait_recv()

        @pl.when(r < nr - 1)
        def _():
            edge_down(g).wait_send()
            edge_up(g).wait_recv()

    def frame_out(f):
        return pltpu.make_async_copy(og.at[f], out_ig.at[f], osem.at[f])

    def backward(f, z):
        taps(bpad, f, range(rd // 2), wb, z)

    def settle(f, z):
        for i in range(rd):
            og[f, i] = (gpad[f, i].astype(F32) + joined(z, i, (1, -1))).astype(BF16)

    def frame(f):
        if f == fd - 3:
            arrived(1)
        if f < fd - 1:
            backward(f + 1, (ya, yb2)[(f + 1) % 2])
        settle(f, (ya, yb2)[f % 2])
        frame_out(f).start()

    arrived(0)
    backward(0, ya)
    go2()
    frame(0)
    frame(1)

    @pl.when(t > 0)
    def _():
        halo.wait_recv()

    @pl.when(t < nt - 1)
    def _():
        halo.wait_send()

    lane8 = lax.broadcasted_iota(jnp.int32, (8, C), 1)
    sub8 = lax.broadcasted_iota(jnp.int32, (8, C), 0)
    count = 24.0 * width
    stats = jnp.zeros((8, C), F32)
    for f in range(fd):
        m = yb[f] + group(yb[f], 1)
        m = m + (group(yb[f - 1], 2) if f >= 1 else 0.0)
        m = m + (group(yb[f - 2], 3) if f >= 2 else 0.0)
        if f < 2:
            m = m + group(hrecv[...], f)
        m = jnp.where(lane < 24, m, 0.0).astype(BF16).astype(F32)
        pix[f * width : (f + 1) * width, :] = m
        mean = jnp.sum(m, keepdims=True) / count
        away = jnp.where(lane < 24, m - mean, 0.0)
        square = jnp.sum(away * away, keepdims=True)
        here = jnp.where(lane8 == 0, mean, jnp.where(lane8 == 1, square, 0.0))
        stats = stats + jnp.where(sub8 == f, here, 0.0)
    stat[r] = stats

    def stat_out(d):
        return remote(stat.at[r], stat.at[r], ss.at[d], sr.at[r], t, lax.rem(r + d, nr))

    def stat_in(d):
        peer = lax.rem(r + d, nr)
        return remote(stat.at[r], stat.at[peer], ss.at[d], sr.at[peer], t, peer)

    for d in range(1, nr):
        stat_out(d).start()

    frame(2)
    go3()
    frame(3)
    frame(4)

    for d in range(1, nr):
        stat_out(d).wait_send()
        stat_in(d).wait_recv()

    for h in range(2):
        wpf[h] = w_patch[:, h * C : (h + 1) * C].astype(F32)
    for v in range(PATCH):
        tap = jnp.concatenate([wpf[h, pl.ds(v, 24, stride=PATCH), :] for h in range(2)], axis=1)
        wv[v] = jnp.concatenate([tap, jnp.zeros((C - 24, 2 * C), F32)], axis=0).astype(BF16)
    every = stat[...]
    means = jnp.sum(jnp.where(lane8 == 0, every, 0.0), axis=2, keepdims=True)
    squares = jnp.sum(jnp.where(lane8 == 1, every, 0.0), axis=2, keepdims=True)
    center = jnp.sum(means, axis=0, keepdims=True) / nr
    apart = means - center
    spread = jnp.sum(squares + count * apart * apart, axis=0, keepdims=True) / (count * nr)
    scale = lax.rsqrt(spread + 1e-05)
    for f in range(fd):
        m = pix[f * width : (f + 1) * width, :]
        m = (m - center[0, f : f + 1, :]) * scale[0, f : f + 1, :]
        pix[f * width : (f + 1) * width, :] = m
    inner = jnp.zeros((fd * width // PATCH, 2 * C), F32)
    for v in range(PATCH):
        taken = pix[pl.ds(v, fd * width // PATCH, stride=PATCH), :]
        inner = inner + mm(taken.astype(BF16), wv[v])
    inner = jnp.where(inner >= 0, inner, 0.2 * inner)
    in_high = inner.astype(BF16)
    in_low = (inner - in_high.astype(F32)).astype(BF16)
    wl = jnp.concatenate([w_logit[0:1], w_logit[1:2]], axis=1)
    wl = jnp.broadcast_to(wl, (8, 2 * C)).astype(BF16)
    lgs[r] = mm_nt(wl, in_high) + mm_nt(wl, in_low)

    def lg_out(d):
        return remote(lgs.at[r], lgs.at[r], ls.at[d], lr.at[r], t, lax.rem(r + d, nr))

    def lg_in(d):
        peer = lax.rem(r + d, nr)
        return remote(lgs.at[r], lgs.at[peer], ls.at[d], lr.at[peer], t, peer)

    for d in range(1, nr):
        lg_out(d).start()

    go4()
    frame(5)
    frame(6)
    frame(7)
    go5()

    for d in range(1, nr):
        lg_out(d).wait_send()
        lg_in(d).wait_recv()
    table = jnp.concatenate([lgs[i, 0:1, :] for i in range(nr)], axis=0)
    out_lg[0] = pltpu.roll(table, lax.rem(C - 16 * r, C), 1)[:, 0:16]

    finish_sums()
    for f in range(fd):
        frame_out(f).wait()


def hand_over(*refs):
    ins, outs, held, sem = refs[0:4], refs[4:8], refs[8:12], refs[12]
    fd = ins[0].shape[0]
    routes = [(ins[0].at[f], held[0].at[f], outs[0].at[f]) for f in range(fd)]
    routes += [(ins[i], held[i], outs[i]) for i in range(1, 4)]
    loads = [pltpu.make_async_copy(a, b, sem.at[0, i]) for i, (a, b, c) in enumerate(routes)]
    stores = [pltpu.make_async_copy(b, c, sem.at[1, i]) for i, (a, b, c) in enumerate(routes)]
    for load in loads:
        load.start()
    for load, store in zip(loads, stores):
        load.wait()
        store.start()
    for store in stores:
        store.wait()


def shards(video, w_space, w_time, w_pixel, w_patch, w_logit, grad_out):
    fd, rd, width, chans = video.shape
    nt = lax.axis_size("tm")
    nr = lax.axis_size("rows")
    hbm = pl.BlockSpec(memory_space=pltpu.HBM)
    vmem = pl.BlockSpec(memory_space=pltpu.VMEM)
    dma = pltpu.SemaphoreType.DMA
    piece = 6 * chans // nt
    scratch = [
        pltpu.VMEM((fd, rd + 2, width, chans), BF16),
        pltpu.VMEM((fd + 2, rd, width, chans), BF16),
        pltpu.VMEM((fd, rd, width, chans), BF16),
        pltpu.VMEM((fd, rd + 2, width, chans), BF16),
        pltpu.VMEM((fd, rd, width, chans), BF16),
        pltpu.VMEM((fd, rd, width, chans), BF16),
        pltpu.VMEM((fd, rd + 2, chans, width), BF16),
        pltpu.VMEM((fd, rd, chans, width), BF16),
        pltpu.VMEM((fd, rd * width, chans), F32),
        pltpu.VMEM((fd, rd, width, chans), BF16),
        pltpu.VMEM((3, 4, LINE, chans), F32),
        pltpu.VMEM((3, 4, LINE, chans), F32),
        pltpu.VMEM((4, LINE, chans), F32),
        pltpu.VMEM((4, LINE, chans), F32),
        pltpu.VMEM((3, rd, LINE, chans), F32),
        pltpu.VMEM((3, rd, LINE, chans), F32),
        pltpu.VMEM((3, 4 * chans, 2 * chans), BF16),
        pltpu.VMEM((3, 4 * chans, 2 * chans), BF16),
        pltpu.VMEM((4 * chans, 2 * chans), BF16),
        pltpu.VMEM((PATCH, 2 * chans, 2 * chans), BF16),
        pltpu.VMEM((2, 192, chans), F32),
        pltpu.VMEM((PATCH, chans, 2 * chans), BF16),
        pltpu.VMEM((4, chans, chans), F32),
        pltpu.VMEM((3, 3, chans, chans), BF16),
        pltpu.VMEM((3, chans, chans), BF16),
        pltpu.VMEM((3, chans), BF16),
        pltpu.VMEM((192, 2 * chans), BF16),
        pltpu.VMEM((2, chans), BF16),
        pltpu.VMEM((fd, width, chans), F32),
        pltpu.VMEM((width, chans), F32),
        pltpu.VMEM((width, chans), F32),
        pltpu.VMEM((nr, 8, chans), F32),
        pltpu.VMEM((nr, 8, chans), F32),
        pltpu.VMEM((fd * width, chans), F32),
        pltpu.VMEM((12, chans, chans), F32),
        pltpu.VMEM((6, chans, chans), F32),
        pltpu.VMEM((nt, piece, chans), BF16),
        pltpu.VMEM((nt, piece, chans), BF16),
        pltpu.VMEM((nr // 2, piece, chans), F32),
        pltpu.VMEM((2, nt, piece, chans), BF16),
        dma((2,)), dma((fd,)), dma((5,)),
        dma((2, 2)), dma((2, 2)), dma((1,)), dma((1,)), dma((2, 2)), dma((2, 2)),
        dma((1,)), dma((1,)), dma((nr,)), dma((nr,)), dma((nr,)), dma((nr,)),
        dma((1,)), dma((1,)), dma((nt,)), dma((nt,)), dma((nr // 2,)), dma((nr // 2,)),
        dma((nt,)), dma((nt,)), dma((1,)), dma((1,)),
    ]
    factor = 1.0 / math.sqrt(fd * rd * width * nt * nr)
    results = pl.pallas_call(
        functools.partial(kernel, nt, nr, factor),
        out_shape=(
            jax.ShapeDtypeStruct(video.shape, BF16),
            jax.ShapeDtypeStruct((3, 3, chans, chans), F32),
            jax.ShapeDtypeStruct((3, chans, chans), F32),
            jax.ShapeDtypeStruct((fd // nr, nr, width // PATCH), F32),
        ),
        in_specs=[hbm] * 7,
        out_specs=(pl.BlockSpec(memory_space=pl.ANY), vmem, vmem, vmem),
        scratch_shapes=scratch,
        compiler_params=pltpu.CompilerParams(
            collective_id=0, has_side_effects=True, vmem_limit_bytes=60 * 1024 * 1024
        ),
        cost_estimate=pl.CostEstimate(
            flops=2 * fd * rd * width * chans * chans * 36,
            bytes_accessed=3 * fd * rd * width * chans * 2,
            transcendentals=fd * rd * width * chans,
        ),
        name="block_step",
    )(video, w_space, w_time, w_pixel, w_patch, w_logit.reshape(2, chans), grad_out)
    anywhere = pl.BlockSpec(memory_space=pl.ANY)
    return pl.pallas_call(
        hand_over,
        out_shape=[jax.ShapeDtypeStruct(x.shape, x.dtype) for x in results],
        in_specs=[anywhere] * 4,
        out_specs=[anywhere] * 4,
        scratch_shapes=[pltpu.VMEM(x.shape, x.dtype) for x in results] + [dma((2, fd + 3))],
        name="hand_over",
    )(*results)


def solution(mesh):
    in_specs = (P("tm", "rows", None, None), P(), P(), P(), P(), P(), P("tm", "rows", None, None))
    out_specs = (P("tm", "rows", None, None), P(), P(), P(("tm", "rows"), None, None))
    return jax.shard_map(shards, mesh=mesh, in_specs=in_specs, out_specs=out_specs, check_vma=False)
```

time: 61 us -> 51.7 us (0.85)
  local copies, waits for them, and re-layouts: 5.52 us -> 0 us
  Pallas kernels: 53.5 us -> 50.9 us
  other arithmetic: 1.18 us -> 0 us
    reshape x2 -> x0, local copies, waits for them, and re-layouts: 2.65 us -> none  [the longest x1 1.43 us: shards(): logits = lg[:, 0:16].reshape(1, nr, 16)]
    pallas_call x1 -> x2, Pallas kernels: 53.5 us -> 50.9 us  [the longest x1 48.2 us: shards(): pl.pallas_call(functools.partial(kernel, nt, nr, factor), out_shape=(jax....]
    slice x2 -> x0, local copies, waits for them, and re-layouts: 1.55 us -> none  [shards(): return (ig, sums[0:9].reshape(3, 3, chans, chans), sums[9:12], logits)]
    unnamed x3 -> x0, local copies, waits for them, and re-layouts: 1.32 us -> none
    mul x1 -> x0, other arithmetic: 1.18 us -> none  [shards(): ar.reshape(12, chans, chans) * (1.0 / math.sqrt(fd * rd * width * nt * nr))]
where the time goes in v2:
time: 51.7 us; the launch traced here: 51.6 us
  Pallas kernels  50.9 us (98%)
  between operations  0.64 us (1%)
    pallas_call x1, Pallas kernels, shards(): pl.pallas_call(functools.partial(kernel, nt, nr, factor), out_shape=(jax....  48.2 us
    pallas_call x1, Pallas kernels, shards(): pl.pallas_call(hand_over, out_shape=[jax.ShapeDtypeStruct(x.shape, x.dtyp...  2.77 us

profile of v2, /device:TPU:1, one launch (start us, length us, event | category | flops | bytes accessed | tf_op | source)
XLA Modules:
  0.0 51.6 jit_solution(1998660239851693503)
XLA Ops:
  0.6 48.2 %block_step.1 = (bf16[8,8,128,128]{3,2,1,0:T(8,128)(2,1)}, f32[3,3,128,128]{3,2,1,0:T(8,128)}, f32[3,128,128]{2,1,0:T(8,128)}, f32[1,8,16]{2,1,0:T(8,128)}) custom-call(bf16[8,8,128,128]{3,2,1,0:T(8,128)(2,1)} %video.1, bf16[3,3,128,128]{3,2,1,0:T(8,128)(2,1)} %w_space_in.1, bf16[3,128,128]{2,1,0:T(8,128)(2,1)} %w_time_in.1, bf16[3,128]{1,0:T(4,128)(2,1)} %w_pixel_in.1, ...), custom_call_target="tpu_custom_call" | custom-call | flops 9663676416 | bytes 6291456 | tf_op jit(solution)/shard_map/block_step/pallas_call | solution.py:615
  48.8 2.8 %hand_over.1 = (bf16[8,8,128,128]{3,2,1,0:T(8,128)(2,1)}, f32[3,3,128,128]{3,2,1,0:T(8,128)}, f32[3,128,128]{2,1,0:T(8,128)}, f32[1,8,16]{2,1,0:T(8,128)}) custom-call(bf16[8,8,128,128]{3,2,1,0:T(8,128)(2,1)} %get-tuple-element.8.refs_0_, f32[3,3,128,128]{3,2,1,0:T(8,128)} %get-tuple-element.9.refs_1_, f32[3,128,128]{2,1,0:T(8,128)} %get-tuple-element.10.refs_2_, ...), custom_call_target="tpu_custom_call" | custom-call | tf_op jit(solution)/shard_map/hand_over/pallas_call | solution.py:637

commit v3 on v2

--- a/solution.py
+++ b/solution.py
@@ -70,6 +70,37 @@
     load_g.start()
     load_v.start()
 
+    pl.semaphore_wait(barrier, nr - 1 + nt - 1)
+
+    parts = (pl.ds(0, 3), pl.ds(3, fd - 3))
+    to_up = [
+        remote(video.at[at, 0], vpad.at[at, rd + 1], vs.at[0, e], vr.at[0, e], t, above)
+        for e, at in enumerate(parts)
+    ]
+    to_down = [
+        remote(video.at[at, rd - 1], vpad.at[at, 0], vs.at[1, e], vr.at[1, e], t, below)
+        for e, at in enumerate(parts)
+    ]
+    to_prev = [
+        remote(grad.at[e], gpad.at[fd + e], gs.at[e], gr.at[e], jnp.maximum(t - 1, 0), r)
+        for e in range(2)
+    ]
+
+    for e in range(2):
+        @pl.when(r > 0)
+        def _():
+            to_up[e].start()
+
+        @pl.when(r < nr - 1)
+        def _():
+            to_down[e].start()
+
+    @pl.when(t > 0)
+    def _():
+        to_prev[0].start()
+        to_prev[1].start()
+
+
     edge = jnp.zeros((8, C), F32)
     for z in (za, zb, ya, yb2):
         for dj in range(3):
@@ -93,32 +124,6 @@
             for dj in range(3):
                 wf[(dj,) + at] = w_space[lag, dj] * 0.5 if 0 <= lag <= 2 else blank
 
-    pl.semaphore_wait(barrier, nr - 1 + nt - 1)
-
-    parts = (pl.ds(0, 3), pl.ds(3, fd - 3))
-    to_up = [
-        remote(video.at[at, 0], vpad.at[at, rd + 1], vs.at[0, e], vr.at[0, e], t, above)
-        for e, at in enumerate(parts)
-    ]
-    to_down = [
-        remote(video.at[at, rd - 1], vpad.at[at, 0], vs.at[1, e], vr.at[1, e], t, below)
-        for e, at in enumerate(parts)
-    ]
-    to_prev = remote(grad.at[0:2], gpad.at[fd : fd + 2], gs.at[0], gr.at[0], jnp.maximum(t - 1, 0), r)
-
-    for e in range(2):
-        @pl.when(r > 0)
-        def _():
-            to_up[e].start()
-
-        @pl.when(r < nr - 1)
-        def _():
-            to_down[e].start()
-
-    @pl.when(t > 0)
-    def _():
-        to_prev.start()
-
     @pl.when(r == 0)
     def _():
         vpad[:, 0] = jnp.zeros((fd, width, C), BF16)
@@ -150,15 +155,24 @@
     load_v.wait()
 
     def taps(src, f, starts, w, z):
-        lhs = jnp.concatenate(
-            [jnp.concatenate([src[f, 2 * p + a] for p in starts], axis=0) for a in range(4)], axis=1
-        )
-        for dj in range(3):
+        def tap(dj):
+            lhs = jnp.concatenate(
+                [jnp.concatenate([src[f, 2 * p + a] for p in starts], axis=0) for a in range(4)], axis=1
+            )
             part = mm(lhs, w[dj])
             for k in range(len(starts)):
                 for o in range(2):
                     z[dj, 2 * k + o, 8 : C + 8] = part[k * C : (k + 1) * C, o * C : (o + 1) * C]
 
+        return [functools.partial(tap, dj) for dj in range(3)]
+
+    def in_turns(first, second):
+        count = len(first)
+        for n, work in enumerate(first):
+            work()
+            for other in second[n * len(second) // count : (n + 1) * len(second) // count]:
+                other()
+
     def joined(z, q, steps):
         mid = z[1, q, 8 : C + 8]
         return mid + z[0, q, 8 + steps[0] : C + 8 + steps[0]] + z[2, q, 8 + steps[1] : C + 8 + steps[1]]
@@ -187,42 +201,63 @@
 
     def place(u):
         last = u // (2 * late)
-        f = (1 - last) * lax.rem(u, late) + last * (late + lax.rem(u, 2))
-        outer = (1 - last) * (u // late) + last * lax.rem(u // 2, 2)
+        f = (1 - last) * lax.rem(u, late) + last * (late + lax.rem(u // 2, 2))
+        outer = (1 - last) * (u // late) + last * lax.rem(u, 2)
         return f, outer, (1 - outer, 2 + outer)
 
     def forward(u, z):
         f, _, starts = place(u)
-        taps(vpad, f, starts, wf, z)
+        return taps(vpad, f, starts, wf, z)
 
     def activate(u, z, line):
-        f, outer, starts = place(u)
-        for k in range(2):
-            for o in range(2):
-                q = 2 * k + o
-                i = 2 * starts[k] + o
-                x = joined(z, q, (-1, 1))
-                th = jnp.tanh(x)
-                up = 1.0 + th
-                h = x * up
-                hb = h.astype(BF16)
-                hid[f, i] = hb
-                htr[f, i] = hb.T
-                b = bh[f, pl.ds(i * C, C), :] * (up + h * (1.0 - th))
-                line[q, 8 : C + 8] = b
-                bpad[f, i + 1] = b.astype(BF16)
-                bleft[f, i] = line[q, 9 : C + 9].astype(BF16)
-                bright[f, i] = line[q, 7 : C + 7].astype(BF16)
-                vtr[f, i + 1] = vpad[f, i + 1].T
+        f, _, starts = place(u)
+
+        def one(q):
+            i = 2 * starts[q // 2] + q % 2
+            x = joined(z, q, (-1, 1))
+            th = jnp.tanh(x)
+            up = 1.0 + th
+            h = x * up
+            hb = h.astype(BF16)
+            hid[f, i] = hb
+            htr[f, i] = hb.T
+            b = bh[f, pl.ds(i * C, C), :] * (up + h * (1.0 - th))
+            line[q, 8 : C + 8] = b
+            bpad[f, i + 1] = b.astype(BF16)
+            bleft[f, i] = line[q, 9 : C + 9].astype(BF16)
+            bright[f, i] = line[q, 7 : C + 7].astype(BF16)
+            vtr[f, i + 1] = vpad[f, i + 1].T
+
+        return [functools.partial(one, q) for q in range(4)]
+
+    def outer_rows(u):
+        f, outer, _ = place(u)
 
         @pl.when(outer == 1)
         def _():
             vtr[f, 0] = vpad[f, 0].T
             vtr[f, rd + 1] = vpad[f, rd + 1].T
 
+    def back_hidden_late(e):
+        @pl.when(t > 0)
+        def _():
+            to_prev[e].wait_send()
+
+        @pl.when(t < nt - 1)
+        def _():
+            to_prev[e].wait_recv()
+
+        f = late + e
+        lhs = jnp.concatenate([gpad[f + a].reshape(rd * width, C) for a in range(3)], axis=1)
+        bh[f] = mm(lhs, wt[0 : 3 * C, 0:C])
+
     def two_units(k, carry):
-        forward(2 * k + 1, zb)
-        activate(2 * k, za, line_a)
+        @pl.when(k == units // 2 - 1)
+        def _():
+            back_hidden_late(1)
+
+        in_turns(forward(2 * k + 1, zb), activate(2 * k, za, line_a))
+        outer_rows(2 * k)
 
         for e in range(2):
             @pl.when(k == late // 2 - 1 + e)
@@ -237,8 +272,10 @@
                     to_down[e].wait_send()
                     to_up[e].wait_recv()
 
-        forward(jnp.minimum(2 * k + 2, units - 1), za)
-        activate(2 * k + 1, zb, line_b)
+        in_turns(
+            forward(jnp.minimum(2 * k + 2, units - 1), za), activate(2 * k + 1, zb, line_b)
+        )
+        outer_rows(2 * k + 1)
         return carry
 
     mine = pl.ds(6 * core, 6)
@@ -249,28 +286,22 @@
 
     def sum2(d):
         peer = lax.rem(t + d, nt)
-        return remote(s1.at[peer], s2.at[t], s2s.at[d], s2r.at[t], peer, r)
-
-    def sum2_in(d):
-        peer = lax.rem(t + d, nt)
-        return remote(s1.at[t], s2.at[peer], s2s.at[d], s2r.at[peer], peer, r)
+        return remote(s1.at[peer], s2.at[t], s2s.at[0], s2r.at[0], peer, r)
+
+    all2 = remote(s1.at[0 : nt - 1], s2.at[0 : nt - 1], s2s.at[0], s2r.at[0], t, partner)
 
     def sum3(d):
         peer = lax.rem(xpos + d, nx)
-        return remote(s3.at[xpos], s3.at[xpos], s3s.at[d], s3r.at[xpos], t, 2 * peer + core)
-
-    def sum3_in(d):
-        peer = lax.rem(xpos + d, nx)
-        return remote(s3.at[xpos], s3.at[peer], s3s.at[d], s3r.at[peer], t, 2 * peer + core)
+        return remote(s3.at[xpos], s3.at[xpos], s3s.at[0], s3r.at[0], t, 2 * peer + core)
+
+    all3 = remote(s3.at[0 : nx - 1], s3.at[0 : nx - 1], s3s.at[0], s3r.at[0], t, partner)
 
     def back4(d):
         return remote(
-            ob.at[core, t], ob.at[core, t], s4s.at[d], s4r.at[t], lax.rem(t + d, nt), r
+            ob.at[core, t], ob.at[core, t], s4s.at[0], s4r.at[0], lax.rem(t + d, nt), r
         )
 
-    def back4_in(d):
-        peer = lax.rem(t + d, nt)
-        return remote(ob.at[core, t], ob.at[core, peer], s4s.at[d], s4r.at[peer], peer, r)
+    all4 = remote(ob.at[core, 0 : nt - 1], ob.at[core, 0 : nt - 1], s4s.at[0], s4r.at[0], t, partner)
 
     back5 = remote(ob.at[core], ob.at[core], s5s.at[0], s5r.at[0], t, partner)
     back5_in = remote(ob.at[core], ob.at[1 - core], s5s.at[0], s5r.at[0], t, partner)
@@ -283,25 +314,19 @@
         s2[t] = s1[t]
 
     def go3():
-        for d in range(1, nt):
-            sum2(d).wait_send()
-            sum2_in(d).wait_recv()
+        all2.wait_recv()
         s3[xpos] = jnp.sum(s2[...].astype(F32), axis=0)
         for d in range(1, nx):
             sum3(d).start()
 
     def go4():
-        for d in range(1, nx):
-            sum3(d).wait_send()
-            sum3_in(d).wait_recv()
+        all3.wait_recv()
         ob[core, t] = (jnp.sum(s3[...], axis=0) * factor).astype(BF16)
         for d in range(1, nt):
             back4(d).start()
 
     def go5():
-        for d in range(1, nt):
-            back4(d).wait_send()
-            back4_in(d).wait_recv()
+        all4.wait_recv()
         back5.start()
 
     def finish_sums():
@@ -338,20 +363,12 @@
             acc[9 + k] += tg[:, k * C : (k + 1) * C]
         return carry
 
-    forward(0, za)
+    in_turns(forward(0, za), [])
     lax.fori_loop(0, late, two_units, 0)
     send_edges(0)
     lax.fori_loop(0, late // 2, grads, 0)
 
-    @pl.when(t > 0)
-    def _():
-        to_prev.wait_send()
-
-    @pl.when(t < nt - 1)
-    def _():
-        to_prev.wait_recv()
-
-    back_hidden(late)
+    back_hidden_late(0)
     lax.fori_loop(late, units // 2, two_units, 0)
     send_edges(1)
     grads(late // 2, 0)
@@ -420,22 +437,27 @@
         return pltpu.make_async_copy(og.at[f], out_ig.at[f], osem.at[f])
 
     def backward(f, z):
-        taps(bpad, f, range(rd // 2), wb, z)
+        return taps(bpad, f, range(rd // 2), wb, z)
 
     def settle(f, z):
-        for i in range(rd):
+        def one(i):
             og[f, i] = (gpad[f, i].astype(F32) + joined(z, i, (1, -1))).astype(BF16)
+
+        return [functools.partial(one, i) for i in range(rd)]
 
     def frame(f):
         if f == fd - 3:
             arrived(1)
+        lines = settle(f, (ya, yb2)[f % 2])
         if f < fd - 1:
-            backward(f + 1, (ya, yb2)[(f + 1) % 2])
-        settle(f, (ya, yb2)[f % 2])
+            in_turns(backward(f + 1, (ya, yb2)[(f + 1) % 2]), lines)
+        else:
+            for line in lines:
+                line()
         frame_out(f).start()
 
     arrived(0)
-    backward(0, ya)
+    in_turns(backward(0, ya), [])
     go2()
     frame(0)
     frame(1)
@@ -468,11 +490,9 @@
     stat[r] = stats
 
     def stat_out(d):
-        return remote(stat.at[r], stat.at[r], ss.at[d], sr.at[r], t, lax.rem(r + d, nr))
-
-    def stat_in(d):
-        peer = lax.rem(r + d, nr)
-        return remote(stat.at[r], stat.at[peer], ss.at[d], sr.at[peer], t, peer)
+        return remote(stat.at[r], stat.at[r], ss.at[0], sr.at[0], t, lax.rem(r + d, nr))
+
+    all_stat = remote(stat.at[0 : nr - 1], stat.at[0 : nr - 1], ss.at[0], sr.at[0], t, partner)
 
     for d in range(1, nr):
         stat_out(d).start()
@@ -482,9 +502,7 @@
     frame(3)
     frame(4)
 
-    for d in range(1, nr):
-        stat_out(d).wait_send()
-        stat_in(d).wait_recv()
+    all_stat.wait_recv()
 
     for h in range(2):
         wpf[h] = w_patch[:, h * C : (h + 1) * C].astype(F32)
@@ -514,11 +532,9 @@
     lgs[r] = mm_nt(wl, in_high) + mm_nt(wl, in_low)
 
     def lg_out(d):
-        return remote(lgs.at[r], lgs.at[r], ls.at[d], lr.at[r], t, lax.rem(r + d, nr))
-
-    def lg_in(d):
-        peer = lax.rem(r + d, nr)
-        return remote(lgs.at[r], lgs.at[peer], ls.at[d], lr.at[peer], t, peer)
+        return remote(lgs.at[r], lgs.at[r], ls.at[0], lr.at[0], t, lax.rem(r + d, nr))
+
+    all_lg = remote(lgs.at[0 : nr - 1], lgs.at[0 : nr - 1], ls.at[0], lr.at[0], t, partner)
 
     for d in range(1, nr):
         lg_out(d).start()
@@ -529,13 +545,13 @@
     frame(7)
     go5()
 
-    for d in range(1, nr):
-        lg_out(d).wait_send()
-        lg_in(d).wait_recv()
+    all_lg.wait_recv()
     table = jnp.concatenate([lgs[i, 0:1, :] for i in range(nr)], axis=0)
     out_lg[0] = pltpu.roll(table, lax.rem(C - 16 * r, C), 1)[:, 0:16]
 
     finish_sums()
+    for step in (all2, all3, all4, all_stat, all_lg):
+        step.wait_send()
     for f in range(fd):
         frame_out(f).wait()
 
@@ -606,7 +622,7 @@
         pltpu.VMEM((nr // 2, piece, chans), F32),
         pltpu.VMEM((2, nt, piece, chans), BF16),
         dma((2,)), dma((fd,)), dma((5,)),
-        dma((2, 2)), dma((2, 2)), dma((1,)), dma((1,)), dma((2, 2)), dma((2, 2)),
+        dma((2, 2)), dma((2, 2)), dma((2,)), dma((2,)), dma((2, 2)), dma((2, 2)),
         dma((1,)), dma((1,)), dma((nr,)), dma((nr,)), dma((nr,)), dma((nr,)),
         dma((1,)), dma((1,)), dma((nt,)), dma((nt,)), dma((nr // 2,)), dma((nr // 2,)),
         dma((nt,)), dma((nt,)), dma((1,)), dma((1,)),

time: 51.7 us -> 51.5 us (level)
  no operation moved by 1% of the time
where the time goes in v3:
time: 51.5 us; the launch traced here: 51.4 us
  Pallas kernels  50.8 us (99%)
  between operations  0.64 us (1%)
    pallas_call x1, Pallas kernels, shards(): pl.pallas_call(functools.partial(kernel, nt, nr, factor), out_shape=(jax....  48 us
    pallas_call x1, Pallas kernels, shards(): pl.pallas_call(hand_over, out_shape=[jax.ShapeDtypeStruct(x.shape, x.dtyp...  2.77 us

profile of v3, /device:TPU:1, one launch (start us, length us, event | category | flops | bytes accessed | tf_op | source)
XLA Modules:
  0.0 51.4 jit_solution(8489000411099278288)
XLA Ops:
  0.6 48.0 %block_step.1 = (bf16[8,8,128,128]{3,2,1,0:T(8,128)(2,1)}, f32[3,3,128,128]{3,2,1,0:T(8,128)}, f32[3,128,128]{2,1,0:T(8,128)}, f32[1,8,16]{2,1,0:T(8,128)}) custom-call(bf16[8,8,128,128]{3,2,1,0:T(8,128)(2,1)} %video.1, bf16[3,3,128,128]{3,2,1,0:T(8,128)(2,1)} %w_space_in.1, bf16[3,128,128]{2,1,0:T(8,128)(2,1)} %w_time_in.1, bf16[3,128]{1,0:T(4,128)(2,1)} %w_pixel_in.1, ...), custom_call_target="tpu_custom_call" | custom-call | flops 9663676416 | bytes 6291456 | tf_op jit(solution)/shard_map/block_step/pallas_call | solution.py:631
  48.6 2.8 %hand_over.1 = (bf16[8,8,128,128]{3,2,1,0:T(8,128)(2,1)}, f32[3,3,128,128]{3,2,1,0:T(8,128)}, f32[3,128,128]{2,1,0:T(8,128)}, f32[1,8,16]{2,1,0:T(8,128)}) custom-call(bf16[8,8,128,128]{3,2,1,0:T(8,128)(2,1)} %get-tuple-element.8.refs_0_, f32[3,3,128,128]{3,2,1,0:T(8,128)} %get-tuple-element.9.refs_1_, f32[3,128,128]{2,1,0:T(8,128)} %get-tuple-element.10.refs_2_, ...), custom_call_target="tpu_custom_call" | custom-call | tf_op jit(solution)/shard_map/hand_over/pallas_call | solution.py:653
